TPU v7x, 512 devices: a whole 4x4x16 slice. The times are simulated.
512 devices in a mesh: pipe: 2 (over z_hi), ctx: 64 (over y, z_lo, core), tp: 4 (over x).
Axes of the slice: x: 4, y: 4, z: 16 (z_hi: 2, z_lo: 8; z = z_hi * 8 + z_lo), core: 2. Of those that a mesh axis runs over, the one named last changes fastest.
Arguments:
- section_output: bfloat16 [2, 8192, 8192], P('pipe', 'ctx', 'tp'), may hold values from -26 to 26
- norm_gain: float32 [2, 8192], P('pipe'), may hold values from 0.1 to 1.9
- kv_weight: bfloat16 [2, 8192, 1024], P('pipe', 'ctx', 'tp'), may hold values from -0.0625 to 0.0625
- queries: bfloat16 [2, 8192, 4096], P('pipe', 'ctx', 'tp'), may hold values from -171 to 171
- rank_block: int32 [128], replicated, may hold values from 0 to 127, each once
Outputs:
- attention: bfloat16 [2, 8192, 4096], P('pipe', 'ctx', 'tp')
- log_total: float32 [2, 8192, 32], P('pipe', 'ctx', 'tp')
Inputs may be any that keep to these rules, and one draw needn't show every extreme that they name: `rank_block`: each of 0 to 127 once.
All inputs are finite; a program needn't handle non-finite values.
Results may differ from a plain program's by a relative error of at most 0.017.
The roundings to bfloat16 on the way count: a program that leaves them out, or rounds other values in their place, can miss the bound.
Values may be sent and summed in bfloat16 or wider, within the bound.
No kernel may reach another device: no remote copies, remote signals or barrier semaphores. Data moves between devices by JAX's collectives and lax.ppermute only.
A program may use at most 128 MiB of HBM per device.

v0:
```python
import math

import jax
import jax.numpy as jnp
from jax import lax
from jax.sharding import PartitionSpec as P

HD = 128


norm_eps = 1e-05
rope_base = 500000.0
mask_fill = -1e30


def passed_along(shard, axis, by):
    peers = lax.axis_size(axis)
    return lax.ppermute(shard, axis, [(i, (i + by) % peers) for i in range(peers)])


def block_positions(rank_block, ctx_count, half_rows):
    block_ids = rank_block.reshape(ctx_count, 2)
    within = jnp.arange(half_rows, dtype=jnp.int32)
    return (block_ids[:, :, None] * half_rows + within[None, None, :]).reshape(-1)


def rotate_keys(raw_keys, positions):
    width = raw_keys.shape[-1]
    half_width = width // 2
    steps_f = jnp.arange(half_width, dtype=jnp.float32)
    inv_freq = jnp.exp(steps_f * (-2.0 / width) * math.log(rope_base))
    angles = positions.astype(jnp.float32)[:, None] * inv_freq[None, :]
    cosine = jnp.cos(angles)
    sine_part = jnp.sin(angles)
    first_half = raw_keys[:, :half_width]
    second_half = raw_keys[:, half_width:]
    return jnp.concatenate(
        [
            first_half * cosine - second_half * sine_part,
            second_half * cosine + first_half * sine_part,
        ],
        axis=1,
    )


def body(section_output, norm_gain, kv_weight, queries, rank_block):
    ctx_count = lax.axis_size("ctx")
    tok_rows = section_output.shape[1]
    half_rows = tok_rows // 2
    head_dim = HD
    head_count = queries.shape[2] // head_dim
    score_scale = 1.0 / math.sqrt(head_dim)
    received = passed_along(section_output, "pipe", 1)
    gathered = lax.all_gather(received, "tp", axis=2, tiled=True)[0].astype(jnp.float32)
    mean_sq = jnp.mean(gathered * gathered, axis=-1, keepdims=True)
    normed = (gathered * lax.rsqrt(mean_sq + norm_eps) * norm_gain[0]).astype(jnp.bfloat16)
    projected = jnp.dot(
        normed,
        lax.all_gather(kv_weight, "ctx", axis=1, tiled=True)[0],
        preferred_element_type=jnp.float32,
    )
    all_pos = block_positions(rank_block, ctx_count, half_rows)
    own_pos = lax.dynamic_slice_in_dim(all_pos, lax.axis_index("ctx") * tok_rows, tok_rows)
    keys = rotate_keys(projected[:, :head_dim], own_pos).astype(jnp.bfloat16)
    values = projected[:, head_dim:].astype(jnp.bfloat16)
    key_values = jnp.concatenate([keys, values], axis=1)
    query_rows = queries[0].reshape(tok_rows, head_count, head_dim)
    halves = (
        (query_rows[:half_rows], own_pos[:half_rows]),
        (query_rows[half_rows:], own_pos[half_rows:]),
    )

    def tile_logits(query_part, query_pos, segment, key_pos):
        logits = (
            jnp.einsum(
                "qhd,kd->hqk", query_part, segment[:, :head_dim], preferred_element_type=jnp.float32
            )
            * score_scale
        )
        allowed = key_pos[None, None, :] <= query_pos[None, :, None]
        return (logits, allowed)

    def weighted_sum(att_weights, segment):
        return jnp.einsum(
            "hqk,kd->qhd",
            att_weights,
            segment[:, head_dim:].astype(jnp.float32),
            precision=lax.Precision.HIGHEST,
        )

    start_pair = (
        jnp.full((head_count, half_rows), mask_fill, jnp.float32),
        jnp.zeros((head_count, half_rows), jnp.float32),
    )
    init_totals = (start_pair, start_pair)
    start_accum = jnp.zeros((half_rows, head_count, head_dim), jnp.float32)
    init_outputs = (start_accum, start_accum)
    segment = lax.all_gather(key_values, "ctx", axis=0, tiled=True)
    key_pos = all_pos
    results = []
    for half_idx in range(2):
        query_part, query_pos = halves[half_idx]

        def update(state_in, query_part=query_part, query_pos=query_pos):
            logits, allowed = tile_logits(query_part, query_pos, segment, key_pos)
            logits = jnp.where(allowed, logits, mask_fill)
            row_max = jnp.maximum(state_in[0], jnp.max(logits, axis=-1))
            row_sum = jnp.sum(jnp.exp(logits - row_max[..., None]), axis=-1)
            return (row_max, row_sum)

        results.append(update(init_totals[half_idx]))
    totals = tuple(results)
    log_halves = tuple((running_pair[0] + jnp.log(running_pair[1]) for running_pair in totals))
    output_segment = lax.all_gather(key_values, "ctx", axis=0, tiled=True)
    results = []
    for half_idx in range(2):
        query_part, query_pos = halves[half_idx]
        log_half = log_halves[half_idx]

        def update(accum, query_part=query_part, query_pos=query_pos, log_half=log_half):
            logits, allowed = tile_logits(query_part, query_pos, output_segment, all_pos)
            att_weights = jnp.where(allowed, jnp.exp(logits - log_half[..., None]), 0.0)
            return weighted_sum(att_weights, output_segment)

        results.append(update(init_outputs[half_idx]))
    outputs = tuple(results)
    attention = (
        jnp.concatenate(outputs, axis=0)
        .astype(jnp.bfloat16)
        .reshape(tok_rows, head_count * head_dim)
    )
    log_total = jnp.concatenate(
        [jnp.transpose(log_halves[0]), jnp.transpose(log_halves[1])], axis=0
    )
    return (attention[None], log_total[None])


def solution(mesh):
    return jax.shard_map(
        body,
        mesh=mesh,
        in_specs=(
            P("pipe", "ctx", "tp"),
            P("pipe", None),
            P("pipe", "ctx", "tp"),
            P("pipe", "ctx", "tp"),
            P(),
        ),
        out_specs=(P("pipe", "ctx", "tp"), P("pipe", "ctx", "tp")),
        check_vma=False,
    )
```

profile of v0, /device:TPU:1, one launch (start us, length us, event | category | flops | bytes accessed | tf_op | source)
XLA Modules:
  0.0 424.6 jit_solution(8950425790996297745)
XLA Ops:
  7.2 16.3 %collective-permute-start = (bf16[1,128,2048]{2,1,0:T(8,128)(2,1)}, bf16[1,128,2048]{2,1,0:T(8,128)(2,1)S(1)}, u32[]{:S(2)}, u32[]{:S(2)}) collective-permute-start(bf16[1,128,2048]{2,1,0:T(8,128)(2,1)} %param.5), channel_id=1, source_target_pairs={{0,256},{256,0},{1,257},{257,1},{2,258},{258,2},{3,259},{259,3},{4... | collective-permute-start | bytes 1572872 | tf_op jit(solution)/shard_map/ppermute | solution.py:18
  23.5 15.2 %collective-permute-done = bf16[1,128,2048]{2,1,0:T(8,128)(2,1)S(1)} collective-permute-done((bf16[1,128,2048]{2,1,0:T(8,128)(2,1)}, bf16[1,128,2048]{2,1,0:T(8,128)(2,1)S(1)}, u32[]{:S(2)}, u32[]{:S(2)}) %collective-permute-start) | collective-permute-done | bytes 524320 | tf_op jit(solution)/shard_map/ppermute | solution.py:18
  38.7 0.8 copy-done.1
  39.6 0.7 all-gather.6.cloned.1.call-update
  40.3 0.7 broadcast_multiply_fusion
  41.0 0.1 mul.100
  41.1 0.1 iota_add_fusion
  41.5 68.4 %all-gather.4.cloned.1.call-done = bf16[1,128,8192]{2,1,0:T(8,128)(2,1)} async-done(((bf16[1,128,2048]{2,1,0:T(8,128)(2,1)}), bf16[1,128,8192]{2,1,0:T(8,128)(2,1)}) %all-gather.4.cloned.1.call-update) | async-done | bytes 2097168 | tf_op jit(solution)/shard_map/all_gather | solution.py:54
  109.8 2.1 fusion.20
  111.9 123.5 %all-gather.6.cloned.1.call-done = bf16[1,8192,256]{2,1,0:T(8,128)(2,1)} async-done(((bf16[1,128,256]{2,1,0:T(8,128)(2,1)}), bf16[1,8192,256]{2,1,0:T(8,128)(2,1)}) %all-gather.6.cloned.1.call-update) | async-done | bytes 4194320 | tf_op jit(solution)/shard_map/all_gather | solution.py:59
  235.4 3.6 fusion.23
  239.3 0.2 fusion.50
  239.6 0.1 copy.14
  239.7 0.7 pad_maximum_fusion.1
  240.5 1.0 slice_bitcast_fusion.15
  241.6 0.6 broadcast_compare_fusion.1
  242.3 116.9 %all-gather.8.cloned.1.call-done = bf16[8192,256]{1,0:T(8,128)(2,1)} async-done(((bf16[128,256]{1,0:T(8,128)(2,1)}), bf16[8192,256]{1,0:T(8,128)(2,1)}) %all-gather.8.cloned.1.call-update) | async-done | bytes 4194320 | tf_op jit(solution)/shard_map/all_gather | solution.py:114
  359.2 9.1 %fusion.8 = (f32[8,64]{1,0:T(8,128)S(1)}, f32[8192,64,8]{0,1,2:T(8,128)}) fusion(pred[64,8192]{1,0:T(8,128)(4,1)S(1)} %get-tuple-element.10, bf16[64,8,128]{2,1,0:T(8,128)(2,1)S(1)} %bitcast.76, bf16[8192,256]{1,0:T(8,128)(2,1)} %all-gather.8.cloned.1.call-done), kind=kOutput, calls=%fused_computation.12 | convolution fusion | flops 1086324224 | bytes 19531776 | tf_op jit(solution)/shard_map/qhd,kd->hqk/dot_general | solution.py:75
  368.3 3.1 fusion.9
  371.4 16.4 %exponential_reduce_fusion = (f32[8,64]{1,0:T(8,128)S(1)}, f32[8,64]{1,0:T(8,128)S(1)}) fusion(f32[8192,64,8]{0,1,2:T(8,128)S(1)} %get-tuple-element.15, f32[8,64]{1,0:T(8,128)S(1)} %broadcast_maximum_fusion, pred[64,8192]{1,0:T(8,128)(4,1)S(1)} %get-tuple-element.11, f32[8,64]{1,0:T(8,128)S(1)} %broadcast_maximum_fusion.1, ...), kind=kLoop, calls=%fused_computation.10 | loop fusion | flops 33553408 | bytes 34611200 | tf_op jit(solution)/shard_map/reduce_sum | solution.py:108
  387.8 14.0 %fusion.40 = bf16[64,8,128]{2,0,1:T(8,128)(2,1)S(1)} fusion(f32[8192,64,8]{0,1,2:T(8,128)} %get-tuple-element.17, f32[8,64]{1,0:T(8,128)S(1)} %log_add_fusion.1, pred[64,8192]{1,0:T(8,128)(4,1)S(1)} %get-tuple-element.10, bf16[8192,256]{1,0:T(8,128)(2,1)S(1)} %copy-done.2), kind=kOutput, calls=%fused_computation.41 | convolution fusion | flops 6455099392 | bytes 19533824 | tf_op jit(solution)/shard_map/hqk,kd->qhd/dot_general | solution.py:84
  402.1 14.4 %fusion.37 = bf16[64,8,128]{2,0,1:T(8,128)(2,1)S(1)} fusion(f32[8192,64,8]{0,1,2:T(8,128)} %copy-done, f32[8,64]{1,0:T(8,128)S(1)} %log_add_fusion, pred[64,8192]{1,0:T(8,128)(4,1)S(1)} %get-tuple-element.11, bf16[8192,256]{1,0:T(8,128)(2,1)} %all-gather.8.cloned.1.call-done), kind=kOutput, calls=%fused_computation.40 | convolution fusion | flops 6455099392 | bytes 19531776 | tf_op jit(solution)/shard_map/hqk,kd->qhd/dot_general | solution.py:84
  416.7 0.7 pad_maximum_fusion
  417.4 0.7 maximum_bitcast_fusion
  (30 shorter events, 1.1 us)
Async XLA Ops:
  7.2 102.7 %all-gather.4.cloned.1.call-start = ((), (), s32[]{:S(2)}) async-start(), calls=%async_computation | async-start | bytes 2621440 | tf_op jit(solution)/shard_map/all_gather | solution.py:54
  7.2 31.5 %collective-permute-start = (bf16[1,128,2048]{2,1,0:T(8,128)(2,1)}, bf16[1,128,2048]{2,1,0:T(8,128)(2,1)S(1)}, u32[]{:S(2)}, u32[]{:S(2)}) collective-permute-start(bf16[1,128,2048]{2,1,0:T(8,128)(2,1)} %param.5), channel_id=1, source_target_pairs={{0,256},{256,0},{1,257},{257,1},{2,258},{258,2},{3,259},{259,3},{4... | collective-permute-start | bytes 1572872 | tf_op jit(solution)/shard_map/ppermute | solution.py:18
  38.7 0.8 copy-start.1
  39.5 195.9 %all-gather.6.cloned.1.call-start = ((), (), s32[]{:S(2)}) async-start(), calls=%async_computation.1 | async-start | bytes 4259840 | tf_op jit(solution)/shard_map/all_gather | solution.py:59
  40.3 318.9 %all-gather.8.cloned.1.call-start = ((), (), s32[]{:S(2)}) async-start(), calls=%async_computation.2 | async-start | bytes 4259840 | tf_op jit(solution)/shard_map/all_gather | solution.py:114
  359.2 9.1 %copy-start.2 = (bf16[8192,256]{1,0:T(8,128)(2,1)S(1)}, bf16[8192,256]{1,0:T(8,128)(2,1)}, u32[]{:S(2)}) copy-start(bf16[8192,256]{1,0:T(8,128)(2,1)} %all-gather.8.cloned.1.call-done) | copy-start | bytes 12582916
  371.4 16.4 %copy-start = (f32[8192,64,8]{0,1,2:T(8,128)}, f32[8192,64,8]{0,1,2:T(8,128)S(1)}, u32[]{:S(2)}) copy-start(f32[8192,64,8]{0,1,2:T(8,128)S(1)} %get-tuple-element.15) | copy-start | bytes 50331652
Sparse Core Ops, SparseCore 0:
  39.7 70.1 all-gather.3
  112.0 123.3 all-gather.5
  240.6 118.5 all-gather.7
where the time goes:
time: 425 us
  waiting for transfers between devices  325 us (76%)
  matrix products  44.3 us (10%)
  other arithmetic  22.4 us (5%)
  starting transfers between devices  16.4 us (4%)
  between operations  13.9 us (3%)
    all_gather x1, waiting for transfers between devices, body(): lax.all_gather(kv_weight, 'ctx', axis=1, tiled=True)[0]  123 us
    all_gather x1, waiting for transfers between devices, body(): output_segment = lax.all_gather(key_values, 'ctx', axis=0, tiled=True)  117 us
    all_gather x1, waiting for transfers between devices, body(): lax.all_gather(received, 'tp', axis=2, tiled=True)[0].astype(jnp.float32)  68.4 us
    dot_general x2, matrix products, weighted_sum(): jnp.einsum('hqk,kd->qhd', att_weights, segment[:, head_dim:].astype(jnp.f...  28.5 us
    reduce_sum x1, other arithmetic, update(): row_sum = jnp.sum(jnp.exp(logits - row_max[..., None]), axis=-1)  16.4 us
    ppermute x1, starting transfers between devices, passed_along(): lax.ppermute(shard, axis, [(i, (i + by) % peers) for i in range(peers)])  16.3 us
    ppermute x1, waiting for transfers between devices, passed_along(): lax.ppermute(shard, axis, [(i, (i + by) % peers) for i in range(peers)])  15.2 us
    dot_general x2, matrix products, tile_logits(): jnp.einsum('qhd,kd->hqk', query_part, segment[:, :head_dim], preferred_el...  12.2 us
  transfers between devices with their start and end apart: 4, of which 4 were waited for; matrix products, arithmetic and copies ran while one was open for 1% of the time, Pallas kernels for 0%

commit v1 on v0

v1 whole, which is shorter than its diff:
```python
import math

import jax
import jax.numpy as jnp
import numpy as np
from jax import lax
from jax.experimental import pallas as pl
from jax.experimental.pallas import tpu as pltpu
from jax.sharding import Mesh
from jax.sharding import PartitionSpec as P

HD = 128
HEADS = 8
NORM_EPS = 1e-05
ROPE_BASE = 500000.0
NEG = -1e30
SIZES = {"pipe": 2, "y": 4, "zg": 2, "zi": 4, "core": 2, "tp": 4}
AXES = tuple(SIZES)
CTX = ("y", "zg", "zi", "core")
KEY_TILE = 256
VMEM_LIMIT = 56 * 1024 * 1024


def permute(x, axes, move):
    sizes = [SIZES[a] for a in axes]
    pairs = []
    for i in range(int(np.prod(sizes))):
        at = [int(v) for v in np.unravel_index(i, sizes)]
        to = [int(v) % n for v, n in zip(move(*at), sizes)]
        pairs.append((i, int(np.ravel_multi_index(to, sizes))))
    return lax.ppermute(x, axes if len(axes) > 1 else axes[0], pairs)


def spread(unit):
    pair = []
    for u in range(2):
        pair.append(
            permute(
                unit,
                ("pipe", "y", "zg", "zi", "tp"),
                lambda p, y, g, i, t, u=u: (1 - p, t, (i + u) % 2, 3 - (4 * g + i) // 2, y),
            )
        )
    pair = jnp.concatenate(pair, axis=0)
    parts = [pair] + [permute(pair, ("zi",), lambda i, k=k: (i + k,)) for k in (1, 2, 3)]
    own = jnp.stack(parts)
    other = permute(own, ("core",), lambda c: (c + 1,))
    return own, other


def project_kernel(where, acts, sums, gain, own, other, out, weight):
    for from_other, ref in enumerate((own, other)):
        for k in range(4):
            for u in range(2):
                at = where[from_other * 8 + k * 2 + u]
                weight[pl.ds(pl.multiple_of(at * 128, 128), 128), :] = ref[k, u * 128 : (u + 1) * 128, :]
    for y in range(4):
        total = (sums[4 * y] + sums[4 * y + 1]) + (sums[4 * y + 2] + sums[4 * y + 3])
        scale = lax.rsqrt(total * (1.0 / 8192) + NORM_EPS)
        column = jnp.transpose(jnp.broadcast_to(scale[:1], (128, 128)))
        normed = acts[y].astype(jnp.float32) * column[:, :1] * gain[...]
        out[y] = jnp.dot(normed.astype(jnp.bfloat16), weight[...], preferred_element_type=jnp.float32)


def rope_kernel(parts, cos, sin, out):
    total = (parts[0] + parts[1]) + (parts[2] + parts[3])
    raw = total[:, :HD]
    turned = pltpu.roll(raw, HD // 2, 1)
    out[:, :HD] = (raw * cos[...] + turned * sin[...]).astype(jnp.bfloat16)
    out[:, HD:] = total[:, HD:].astype(jnp.bfloat16)


def attend_kernel(meta, q_ref, own, other, out, k_s, v_s, vt_s, q_s, m_s, l_s, acc):
    step = pl.program_id(0)
    rows = HEADS * 64
    factor = math.log2(math.e) / math.sqrt(HD)

    @pl.when(step == 0)
    def _():
        for from_other, ref in enumerate((own, other)):
            for k in range(4):
                for b in range(4):
                    at = pl.multiple_of(meta[from_other * 16 + k * 4 + b] * 64, 64)
                    k_s[pl.ds(at, 64), :] = ref[k, b * 64 : (b + 1) * 64, :HD]
                    v_s[pl.ds(at, 64), :] = ref[k, b * 64 : (b + 1) * 64, HD:]
        for t in range(2048 // KEY_TILE):
            tile = v_s[t * KEY_TILE : (t + 1) * KEY_TILE, :].astype(jnp.float32)
            vt_s[t] = jnp.transpose(tile).astype(jnp.bfloat16)

    for half in range(2):
        for h in range(HEADS):
            q_s[h * 64 : (h + 1) * 64, :] = q_ref[0, half * 64 : (half + 1) * 64, h * HD : (h + 1) * HD]
        before = meta[32 + step * 2 + half]
        has_own = meta[40 + step * 2 + half]
        per_tile = KEY_TILE // 64
        full = before // per_tile
        left = (before - full * per_tile) * 64
        m_s[...] = jnp.full(m_s.shape, NEG, jnp.float32)
        l_s[...] = jnp.zeros(l_s.shape, jnp.float32)
        acc[...] = jnp.zeros(acc.shape, jnp.float32)

        def tile(t, masked):
            keys = k_s[pl.ds(pl.multiple_of(t * KEY_TILE, KEY_TILE), KEY_TILE), :]
            vt = vt_s[t]
            s = lax.dot_general(keys, q_s[...], (((1,), (1,)), ((), ())), preferred_element_type=jnp.float32)
            s = s * factor
            if masked:
                row = lax.broadcasted_iota(jnp.int32, (1, rows), 1)
                limit = left + has_own * ((row & 63) + 1)
                allowed = lax.broadcasted_iota(jnp.int32, (KEY_TILE, rows), 0) < limit
                s = jnp.where(allowed, s, NEG)
            m_old = m_s[:1]
            m_new = jnp.maximum(m_old, jnp.max(s, axis=0, keepdims=True))
            p = jnp.exp2(s - m_new)
            if masked:
                p = jnp.where(allowed, p, 0.0)
            alpha = jnp.exp2(m_old - m_new)
            m_s[:1] = m_new
            l_s[:1] = l_s[:1] * alpha + jnp.sum(p, axis=0, keepdims=True)
            acc[...] = acc[...] * alpha + jnp.dot(vt, p.astype(jnp.bfloat16), preferred_element_type=jnp.float32)

        def whole(t, carry):
            tile(t, False)
            return carry

        lax.fori_loop(0, full, whole, 0)

        @pl.when(left + has_own > 0)
        def _():
            tile(full, True)

        total = l_s[:1]
        some = total > 0.0
        inverse = jnp.where(some, 1.0 / jnp.where(some, total, 1.0), 0.0)
        lse = jnp.where(some, m_s[:1] * math.log(2.0) + jnp.log(jnp.where(some, total, 1.0)), NEG)
        high = lse.astype(jnp.bfloat16).astype(jnp.float32)
        rest = lse - high
        middle = rest.astype(jnp.bfloat16).astype(jnp.float32)
        low = rest - middle
        line = lax.broadcasted_iota(jnp.int32, (128, 128), 0)
        stats = jnp.zeros((64, 128), jnp.float32)
        for pair in range(HEADS // 2):
            cols = slice(pair * 128, (pair + 1) * 128)
            turned = jnp.transpose(acc[:, cols] * inverse[:, cols]).astype(jnp.bfloat16)
            out[0, half * 64 : (half + 1) * 64, (2 * pair) * HD : (2 * pair + 1) * HD] = turned[:64]
            out[0, half * 64 : (half + 1) * 64, (2 * pair + 1) * HD : (2 * pair + 2) * HD] = turned[64:]
            pieces = jnp.where(
                line == 0,
                high[:, cols],
                jnp.where(line == 8, middle[:, cols], jnp.where(line == 16, low[:, cols], 0.0)),
            )
            pieces = jnp.transpose(pieces)
            for odd in range(2):
                head = 2 * pair + odd
                part = pieces[odd * 64 : (odd + 1) * 64]
                stats = stats + (pltpu.roll(part, head, 1) if head else part)
        out[0, half * 64 : (half + 1) * 64, HEADS * HD :] = stats.astype(jnp.bfloat16)


def merge_kernel(parts, out, log_total):
    logs = []
    for i in range(4):
        pieces = parts[i, :, HEADS * HD :].astype(jnp.float32)
        logs.append((pieces + pltpu.roll(pieces, 120, 1)) + pltpu.roll(pieces, 112, 1))
    top = jnp.maximum(jnp.maximum(logs[0], logs[1]), jnp.maximum(logs[2], logs[3]))
    weights = [jnp.exp(v - top) for v in logs]
    total = (weights[0] + weights[1]) + (weights[2] + weights[3])
    log_total[...] = (top + jnp.log(total))[:, :HEADS]
    weights = [w / total for w in weights]
    for h in range(HEADS):
        cols = slice(h * HD, (h + 1) * HD)
        acc = weights[0][:, h : h + 1] * parts[0, :, cols].astype(jnp.float32)
        for i in range(1, 4):
            acc = acc + weights[i][:, h : h + 1] * parts[i, :, cols].astype(jnp.float32)
        out[:, cols] = acc.astype(jnp.bfloat16)


def params(**kw):
    return pltpu.CompilerParams(vmem_limit_bytes=VMEM_LIMIT, **kw)


SMEM = pl.BlockSpec(memory_space=pltpu.SMEM)
VMEM = pl.BlockSpec(memory_space=pltpu.VMEM)


def body(section_output, norm_gain, kv_weight, queries, rank_block):
    y, g, i = lax.axis_index("y"), lax.axis_index("zg"), lax.axis_index("zi")
    c, t = lax.axis_index("core"), lax.axis_index("tp")
    z = g * 4 + i
    acts = section_output[0]

    w_own, w_other = spread(kv_weight[0])
    gain = lax.dynamic_slice(norm_gain, (0, t * 2048), (1, 2048))
    gain = permute(gain, ("pipe", "zg", "zi"), lambda p, a, b: (1 - p, 1 - a, 3 - b))

    square = jnp.sum(jnp.square(acts.astype(jnp.float32)), axis=1)
    square = jnp.broadcast_to(square[None, None, :], (16, 8, 128))
    sums = lax.all_to_all(square, ("y", "tp"), 0, 0, tiled=True)
    acts_y = lax.all_gather(acts, "y", axis=0)
    q_y = lax.all_gather(queries[0], "y", axis=0)

    k_index = jnp.arange(4, dtype=jnp.int32)[:, None]
    u_index = jnp.arange(2, dtype=jnp.int32)[None, :]
    from_z = (2 * (3 - (i - k_index) % 4) + (u_index ^ g)).reshape(-1)
    places = jnp.concatenate([2 * from_z + c, 2 * from_z + 1 - c])

    partial = pl.pallas_call(
        project_kernel,
        out_shape=jax.ShapeDtypeStruct((4, 128, 256), jnp.float32),
        in_specs=[SMEM] + [VMEM] * 5,
        out_specs=VMEM,
        scratch_shapes=[pltpu.VMEM((2048, 256), jnp.bfloat16)],
        compiler_params=params(),
        name="project",
    )(places, acts_y, sums, gain, w_own, w_other)
    partial = lax.all_to_all(partial, "tp", 0, 0, tiled=True)

    half_row = jnp.arange(128, dtype=jnp.int32)
    rank = 16 * t + 2 * z + c
    blocks = lax.dynamic_slice(rank_block, (2 * rank,), (2,))
    pos = jnp.where(half_row < 64, blocks[0], blocks[1]) * 64 + (half_row & 63)
    inv_freq = jnp.exp(jnp.arange(HD // 2, dtype=jnp.float32) * (-2.0 / HD) * math.log(ROPE_BASE))
    angles = pos.astype(jnp.float32)[:, None] * inv_freq[None, :]
    cos, sin = jnp.cos(angles), jnp.sin(angles)
    cos = jnp.concatenate([cos, cos], axis=1)
    sin = jnp.concatenate([-sin, sin], axis=1)
    unit = pl.pallas_call(
        rope_kernel,
        out_shape=jax.ShapeDtypeStruct((128, 256), jnp.bfloat16),
        in_specs=[VMEM] * 3,
        out_specs=VMEM,
        compiler_params=params(),
        name="rope",
    )(partial, cos, sin)
    kv_own, kv_other = spread(unit)

    ranks = 16 * y + places
    ids = rank_block[(2 * ranks[:, None] + jnp.arange(2, dtype=jnp.int32)[None, :]).reshape(-1)]
    order = jnp.sum((ids[None, :] < ids[:, None]).astype(jnp.int32), axis=1)
    q_ranks = 16 * jnp.arange(4, dtype=jnp.int32) + 2 * z + c
    q_ids = rank_block[(2 * q_ranks[:, None] + jnp.arange(2, dtype=jnp.int32)[None, :]).reshape(-1)]
    before = jnp.sum((ids[None, :] < q_ids[:, None]).astype(jnp.int32), axis=1)
    has_own = jnp.sum((ids[None, :] == q_ids[:, None]).astype(jnp.int32), axis=1)
    meta = jnp.concatenate([order, before, has_own])

    rows = HEADS * 64
    width = HEADS * HD + 128
    shares = pl.pallas_call(
        attend_kernel,
        out_shape=jax.ShapeDtypeStruct((4, 128, width), jnp.bfloat16),
        grid_spec=pltpu.PrefetchScalarGridSpec(
            num_scalar_prefetch=1,
            grid=(4,),
            in_specs=[
                pl.BlockSpec((1, 128, HEADS * HD), lambda s, _: (s, 0, 0)),
                pl.BlockSpec((4, 256, 256), lambda s, _: (0, 0, 0)),
                pl.BlockSpec((4, 256, 256), lambda s, _: (0, 0, 0)),
            ],
            out_specs=pl.BlockSpec((1, 128, width), lambda s, _: (s, 0, 0)),
            scratch_shapes=[
                pltpu.VMEM((2048, HD), jnp.bfloat16),
                pltpu.VMEM((2048, HD), jnp.bfloat16),
                pltpu.VMEM((2048 // KEY_TILE, HD, KEY_TILE), jnp.bfloat16),
                pltpu.VMEM((rows, HD), jnp.bfloat16),
                pltpu.VMEM((8, rows), jnp.float32),
                pltpu.VMEM((8, rows), jnp.float32),
                pltpu.VMEM((HD, rows), jnp.float32),
            ],
        ),
        compiler_params=params(),
        name="attend",
    )(meta, q_y, kv_own, kv_other)
    shares = lax.all_to_all(shares, "y", 0, 0, tiled=True)
    attention, log_total = pl.pallas_call(
        merge_kernel,
        out_shape=(
            jax.ShapeDtypeStruct((128, HEADS * HD), jnp.bfloat16),
            jax.ShapeDtypeStruct((128, HEADS), jnp.float32),
        ),
        in_specs=[VMEM],
        out_specs=(VMEM, VMEM),
        compiler_params=params(),
        name="merge",
    )(shares)
    return attention[None], log_total[None]


def solution(mesh):
    fine = Mesh(mesh.devices.reshape(tuple(SIZES.values())), AXES)
    split = P("pipe", CTX, "tp")
    return jax.shard_map(
        body,
        mesh=fine,
        in_specs=(split, P("pipe", None), split, split, P()),
        out_specs=(split, split),
        check_vma=False,
    )
```

time: 425 us -> 192 us (0.45)
  the two profiles are of different devices: /device:TPU:1 before, /device:TPU:129 now
where the time goes in v1:
time: 192 us; the launch traced here: 191 us
  starting transfers between devices  79.3 us (41%)
  Pallas kernels  34.5 us (18%)
  blocking collectives  28.3 us (15%)
  waiting for transfers between devices  21.5 us (11%)
  between operations  14.4 us (8%)
  local copies, waits for them, and re-layouts  7 us (4%)
  other arithmetic  5.62 us (3%)
    ppermute x13, starting transfers between devices, permute(): return lax.ppermute(x, axes if len(axes) > 1 else axes[0], pairs)  65.2 us
    all_to_all x1, blocking collectives, body(): shares = lax.all_to_all(shares, 'y', 0, 0, tiled=True)  28.3 us
    pallas_call x1, Pallas kernels, body(): pl.pallas_call(attend_kernel, out_shape=jax.ShapeDtypeStruct((4, 128, wid...  26.4 us
    ppermute x13, waiting for transfers between devices, permute(): return lax.ppermute(x, axes if len(axes) > 1 else axes[0], pairs)  11.6 us
    all_to_all x1, starting transfers between devices, body(): sums = lax.all_to_all(square, ('y', 'tp'), 0, 0, tiled=True)  9.8 us
    all_to_all x1, waiting for transfers between devices, body(): partial = lax.all_to_all(partial, 'tp', 0, 0, tiled=True)  8.5 us
    all_to_all x1, starting transfers between devices, body(): partial = lax.all_to_all(partial, 'tp', 0, 0, tiled=True)  4.24 us
    unnamed x21, local copies, waits for them, and re-layouts  3.93 us
  transfers between devices with their start and end apart: 17, of which 6 were waited for; matrix products, arithmetic and copies ran while one was open for 5% of the time, Pallas kernels for 3%

profile of v1, /device:TPU:129, one launch (start us, length us, event | category | flops | bytes accessed | tf_op | source)
XLA Modules:
  0.0 190.6 jit_solution(10490307400110453307)
XLA Ops:
  7.9 9.3 %collective-permute-start.1 = (bf16[128,256]{1,0:T(8,128)(2,1)}, bf16[128,256]{1,0:T(8,128)(2,1)S(1)}, u32[]{:S(2)}, u32[]{:S(2)}) collective-permute-start(bf16[128,256]{1,0:T(8,128)(2,1)} %bitcast.27), channel_id=1, source_target_pairs={{0,280},{1,344},{2,408},{3,472},{8,312},{9,376},{10,440},{11,504},... | collective-permute-start | bytes 196616 | tf_op jit(solution)/shard_map/ppermute | solution.py:31
  17.2 5.2 %collective-permute-start.2 = (bf16[128,256]{1,0:T(8,128)(2,1)}, bf16[128,256]{1,0:T(8,128)(2,1)S(1)}, u32[]{:S(2)}, u32[]{:S(2)}) collective-permute-start(bf16[128,256]{1,0:T(8,128)(2,1)} %bitcast.28), channel_id=1, source_target_pairs={{0,312},{1,376},{2,440},{3,504},{8,280},{9,344},{10,408},{11,472},... | collective-permute-start | bytes 196616 | tf_op jit(solution)/shard_map/ppermute | solution.py:31
  22.4 9.3 %collective-permute-start = (f32[1,2048]{1,0:T(1,128)S(1)}, f32[1,2048]{1,0:T(1,128)S(1)}, u32[]{:S(2)}, u32[]{:S(2)}) collective-permute-start(f32[1,2048]{1,0:T(1,128)S(1)} %constant_dynamic-slice_fusion), channel_id=1, source_target_pairs={{0,312},{8,304},{16,296},{24,288},{32,280},{40,272},{48,264},{56,2... | collective-permute-start | bytes 24584 | tf_op jit(solution)/shard_map/ppermute | solution.py:31
  33.6 9.8 %all-to-all-start = ((f32[16,8,128]{2,1,0:T(8,128)}), f32[16,8,128]{2,1,0:T(8,128)S(1)}, u32[]{:S(2)}, u32[]{:S(2)}) async-start(f32[16,8,128]{2,1,0:T(8,128)} %broadcast_in_dim.14), calls=%async_computation | async-start | bytes 131072 | tf_op jit(solution)/shard_map/all_to_all | solution.py:198
  44.3 1.9 %collective-permute-start.3 = (bf16[256,256]{1,0:T(8,128)(2,1)S(1)}, bf16[256,256]{1,0:T(8,128)(2,1)S(1)}, u32[]{:S(2)}, u32[]{:S(2)}) collective-permute-start(bf16[256,256]{1,0:T(8,128)(2,1)S(1)} %constant_dynamic-update-slice_fusion), channel_id=1, source_target_pairs={{0,8},{8,16},{16,24},{24,0},{1,9},{9,17},{17,25},{25,1},{2,10},{10... | collective-permute-start | bytes 393224 | tf_op jit(solution)/shard_map/ppermute | solution.py:31
  46.2 1.9 %collective-permute-start.4 = (bf16[256,256]{1,0:T(8,128)(2,1)S(1)}, bf16[256,256]{1,0:T(8,128)(2,1)S(1)}, u32[]{:S(2)}, u32[]{:S(2)}) collective-permute-start(bf16[256,256]{1,0:T(8,128)(2,1)S(1)} %constant_dynamic-update-slice_fusion), channel_id=1, source_target_pairs={{0,16},{8,24},{16,0},{24,8},{1,17},{9,25},{17,1},{25,9},{2,18},{10... | collective-permute-start | bytes 393224 | tf_op jit(solution)/shard_map/ppermute | solution.py:31
  48.1 5.2 %collective-permute-start.5 = (bf16[256,256]{1,0:T(8,128)(2,1)S(1)}, bf16[256,256]{1,0:T(8,128)(2,1)S(1)}, u32[]{:S(2)}, u32[]{:S(2)}) collective-permute-start(bf16[256,256]{1,0:T(8,128)(2,1)S(1)} %constant_dynamic-update-slice_fusion), channel_id=1, source_target_pairs={{0,24},{8,0},{16,8},{24,16},{1,25},{9,1},{17,9},{25,17},{2,26},{10... | collective-permute-start | bytes 393224 | tf_op jit(solution)/shard_map/ppermute | solution.py:31
  54.3 4.1 %collective-permute-done.4 = bf16[256,256]{1,0:T(8,128)(2,1)S(1)} collective-permute-done((bf16[256,256]{1,0:T(8,128)(2,1)S(1)}, bf16[256,256]{1,0:T(8,128)(2,1)S(1)}, u32[]{:S(2)}, u32[]{:S(2)}) %collective-permute-start.4) | collective-permute-done | bytes 131104 | tf_op jit(solution)/shard_map/ppermute | solution.py:31
  58.8 3.9 %collective-permute-start.6 = (bf16[4,256,256]{2,1,0:T(8,128)(2,1)S(1)}, bf16[4,256,256]{2,1,0:T(8,128)(2,1)S(1)}, u32[]{:S(2)}, u32[]{:S(2)}) collective-permute-start(bf16[4,256,256]{2,1,0:T(8,128)(2,1)S(1)} %pad_maximum_fusion.own), channel_id=1, source_target_pairs={{0,4},{4,0},{1,5},{5,1},{2,6},{6,2},{3,7},{7,3},{8,12},{12,8},{9,1... | collective-permute-start | bytes 1572872 | tf_op jit(solution)/shard_map/ppermute | solution.py:31
  65.8 3.5 %project.1 = f32[4,128,256]{2,1,0:T(8,128)} custom-call(s32[16]{0:T(128)} %get-tuple-element.17.where, bf16[4,128,2048]{2,1,0:T(8,128)(2,1)} %all-gather.5.cloned.1.call-done.acts, f32[16,8,128]{2,1,0:T(8,128)} %copy-done.7, f32[1,2048]{1,0:T(1,128)} %copy-done.8, bf16[4,256,256]{2,1,0:T(8,128)(2,1)} %copy-done.3, bf16[4,256,256]{2,1,0:T(8,128)(2,1)} %copy-done.5), custom_call_target="tpu_custom_call" | custom-call | tf_op jit(solution)/shard_map/project/pallas_call | solution.py:207
  69.3 4.2 %all-to-all-start.1 = ((f32[4,128,256]{2,1,0:T(8,128)}), f32[4,128,256]{2,1,0:T(8,128)S(1)}, u32[]{:S(2)}, u32[]{:S(2)}) async-start(f32[4,128,256]{2,1,0:T(8,128)} %project.1), calls=%async_computation.1 | async-start | bytes 1048576 | tf_op jit(solution)/shard_map/all_to_all | solution.py:216
  74.4 8.5 %all-to-all-done.1.parts = f32[4,128,256]{2,1,0:T(8,128)S(1)} async-done(((f32[4,128,256]{2,1,0:T(8,128)}), f32[4,128,256]{2,1,0:T(8,128)S(1)}, u32[]{:S(2)}, u32[]{:S(2)}) %all-to-all-start.1) | async-done | bytes 524320 | tf_op jit(solution)/shard_map/all_to_all | solution.py:216
  83.7 1.8 rope.1
  85.5 1.9 %collective-permute-start.7 = (bf16[128,256]{1,0:T(8,128)(2,1)}, bf16[128,256]{1,0:T(8,128)(2,1)S(1)}, u32[]{:S(2)}, u32[]{:S(2)}) collective-permute-start(bf16[128,256]{1,0:T(8,128)(2,1)} %rope.1), channel_id=1, source_target_pairs={{0,280},{1,344},{2,408},{3,472},{8,312},{9,376},{10,440},{11,504},... | collective-permute-start | bytes 196616 | tf_op jit(solution)/shard_map/ppermute | solution.py:31
  87.7 12.7 %collective-permute-start.8 = (bf16[128,256]{1,0:T(8,128)(2,1)}, bf16[128,256]{1,0:T(8,128)(2,1)S(1)}, u32[]{:S(2)}, u32[]{:S(2)}) collective-permute-start(bf16[128,256]{1,0:T(8,128)(2,1)} %rope.1), channel_id=1, source_target_pairs={{0,312},{1,376},{2,440},{3,504},{8,280},{9,344},{10,408},{11,472},... | collective-permute-start | bytes 196616 | tf_op jit(solution)/shard_map/ppermute | solution.py:31
  100.4 1.6 collective-permute-done.8
  102.0 3.4 %collective-permute-start.9 = (bf16[256,256]{1,0:T(8,128)(2,1)S(1)}, bf16[256,256]{1,0:T(8,128)(2,1)S(1)}, u32[]{:S(2)}, u32[]{:S(2)}) collective-permute-start(bf16[256,256]{1,0:T(8,128)(2,1)S(1)} %constant_dynamic-update-slice_fusion.2), channel_id=1, source_target_pairs={{0,8},{8,16},{16,24},{24,0},{1,9},{9,17},{17,25},{25,1},{2,10},{10... | collective-permute-start | bytes 393224 | tf_op jit(solution)/shard_map/ppermute | solution.py:31
  105.4 2.8 %collective-permute-start.10 = (bf16[256,256]{1,0:T(8,128)(2,1)S(1)}, bf16[256,256]{1,0:T(8,128)(2,1)S(1)}, u32[]{:S(2)}, u32[]{:S(2)}) collective-permute-start(bf16[256,256]{1,0:T(8,128)(2,1)S(1)} %constant_dynamic-update-slice_fusion.2), channel_id=1, source_target_pairs={{0,16},{8,24},{16,0},{24,8},{1,17},{9,25},{17,1},{25,9},{2,18},{10... | collective-permute-start | bytes 393224 | tf_op jit(solution)/shard_map/ppermute | solution.py:31
  108.2 3.1 %collective-permute-start.11 = (bf16[256,256]{1,0:T(8,128)(2,1)S(1)}, bf16[256,256]{1,0:T(8,128)(2,1)S(1)}, u32[]{:S(2)}, u32[]{:S(2)}) collective-permute-start(bf16[256,256]{1,0:T(8,128)(2,1)S(1)} %constant_dynamic-update-slice_fusion.2), channel_id=1, source_target_pairs={{0,24},{8,0},{16,8},{24,16},{1,25},{9,1},{17,9},{25,17},{2,26},{10... | collective-permute-start | bytes 393224 | tf_op jit(solution)/shard_map/ppermute | solution.py:31
  111.4 4.9 %collective-permute-done.10 = bf16[256,256]{1,0:T(8,128)(2,1)S(1)} collective-permute-done((bf16[256,256]{1,0:T(8,128)(2,1)S(1)}, bf16[256,256]{1,0:T(8,128)(2,1)S(1)}, u32[]{:S(2)}, u32[]{:S(2)}) %collective-permute-start.10) | collective-permute-done | bytes 131104 | tf_op jit(solution)/shard_map/ppermute | solution.py:31
  117.0 4.7 %collective-permute-start.12 = (bf16[4,256,256]{2,1,0:T(8,128)(2,1)S(1)}, bf16[4,256,256]{2,1,0:T(8,128)(2,1)S(1)}, u32[]{:S(2)}, u32[]{:S(2)}) collective-permute-start(bf16[4,256,256]{2,1,0:T(8,128)(2,1)S(1)} %pad_maximum_fusion.1.own), channel_id=1, source_target_pairs={{0,4},{4,0},{1,5},{5,1},{2,6},{6,2},{3,7},{7,3},{8,12},{12,8},{9,1... | collective-permute-start | bytes 1572872 | tf_op jit(solution)/shard_map/ppermute | solution.py:31
  124.8 26.4 %attend.1 = bf16[4,128,1152]{2,1,0:T(8,128)(2,1)} custom-call(s32[48]{0:T(128)} %pad_add_fusion.1.meta, bf16[4,128,1024]{2,1,0:T(8,128)(2,1)} %all-gather.3.cloned.1.call-done.q_ref, bf16[4,256,256]{2,1,0:T(8,128)(2,1)} %copy-done.4, bf16[4,256,256]{2,1,0:T(8,128)(2,1)} %copy-done.6), custom_call_target="tpu_custom_call" | custom-call | tf_op jit(solution)/shard_map/attend/pallas_call | solution.py:248
  151.2 28.3 %all_to_all.15.parts = bf16[4,128,1152]{2,1,0:T(8,128)(2,1)} all-to-all(bf16[4,128,1152]{2,1,0:T(8,128)(2,1)} %attend.1), channel_id=1, replica_groups=mesh['pipe'=2,'y'=4,'zg'=2,'zi'=4,'core'=2,'tp'=4] {'y'}, dimensions={0} | all-to-all | bytes 2359296 | tf_op jit(solution)/shard_map/all_to_all | solution.py:273
  179.5 2.8 %merge.1 = (bf16[128,1024]{1,0:T(8,128)(2,1)}, f32[128,8]{1,0:T(8,128)}) custom-call(bf16[4,128,1152]{2,1,0:T(8,128)(2,1)} %all_to_all.15.parts), custom_call_target="tpu_custom_call" | custom-call | tf_op jit(solution)/shard_map/merge/pallas_call | solution.py:274
  (70 shorter events, 15.1 us)
Async XLA Ops:
  7.2 15.2 %copy-start = (f32[1,8192]{1,0:T(1,128)S(1)}, f32[1,8192]{1,0:T(1,128)}, u32[]{:S(2)}) copy-start(f32[1,8192]{1,0:T(1,128)} %param.6) | copy-start | bytes 98308
  7.2 46.4 %copy-start.1 = (s32[128]{0:T(128)S(1)}, s32[128]{0:T(128)}, u32[]{:S(2)}) copy-start(s32[128]{0:T(128)} %param.9) | copy-start | bytes 1540
  7.2 57.8 %all-gather.5.cloned.1.call-start = ((), (), s32[]{:S(2)}) async-start(), calls=%async_computation.4 | async-start | bytes 2621440 | tf_op jit(solution)/shard_map/all_gather | solution.py:199
  7.9 36.3 %collective-permute-start.1 = (bf16[128,256]{1,0:T(8,128)(2,1)}, bf16[128,256]{1,0:T(8,128)(2,1)S(1)}, u32[]{:S(2)}, u32[]{:S(2)}) collective-permute-start(bf16[128,256]{1,0:T(8,128)(2,1)} %bitcast.27), channel_id=1, source_target_pairs={{0,280},{1,344},{2,408},{3,472},{8,312},{9,376},{10,440},{11,504},... | collective-permute-start | bytes 196616 | tf_op jit(solution)/shard_map/ppermute | solution.py:31
  17.2 27.0 %collective-permute-start.2 = (bf16[128,256]{1,0:T(8,128)(2,1)}, bf16[128,256]{1,0:T(8,128)(2,1)S(1)}, u32[]{:S(2)}, u32[]{:S(2)}) collective-permute-start(bf16[128,256]{1,0:T(8,128)(2,1)} %bitcast.28), channel_id=1, source_target_pairs={{0,312},{1,376},{2,440},{3,504},{8,280},{9,344},{10,408},{11,472},... | collective-permute-start | bytes 196616 | tf_op jit(solution)/shard_map/ppermute | solution.py:31
  22.4 42.5 %collective-permute-start = (f32[1,2048]{1,0:T(1,128)S(1)}, f32[1,2048]{1,0:T(1,128)S(1)}, u32[]{:S(2)}, u32[]{:S(2)}) collective-permute-start(f32[1,2048]{1,0:T(1,128)S(1)} %constant_dynamic-slice_fusion), channel_id=1, source_target_pairs={{0,312},{8,304},{16,296},{24,288},{32,280},{40,272},{48,264},{56,2... | collective-permute-start | bytes 24584 | tf_op jit(solution)/shard_map/ppermute | solution.py:31
  33.6 31.4 %all-to-all-start = ((f32[16,8,128]{2,1,0:T(8,128)}), f32[16,8,128]{2,1,0:T(8,128)S(1)}, u32[]{:S(2)}, u32[]{:S(2)}) async-start(f32[16,8,128]{2,1,0:T(8,128)} %broadcast_in_dim.14), calls=%async_computation | async-start | bytes 131072 | tf_op jit(solution)/shard_map/all_to_all | solution.py:198
  43.4 80.6 %all-gather.3.cloned.1.call-start = ((), (), s32[]{:S(2)}) async-start(), calls=%async_computation.3 | async-start | bytes 1310720 | tf_op jit(solution)/shard_map/all_gather | solution.py:200
  44.3 10.0 %collective-permute-start.3 = (bf16[256,256]{1,0:T(8,128)(2,1)S(1)}, bf16[256,256]{1,0:T(8,128)(2,1)S(1)}, u32[]{:S(2)}, u32[]{:S(2)}) collective-permute-start(bf16[256,256]{1,0:T(8,128)(2,1)S(1)} %constant_dynamic-update-slice_fusion), channel_id=1, source_target_pairs={{0,8},{8,16},{16,24},{24,0},{1,9},{9,17},{17,25},{25,1},{2,10},{10... | collective-permute-start | bytes 393224 | tf_op jit(solution)/shard_map/ppermute | solution.py:31
  46.2 12.2 %collective-permute-start.4 = (bf16[256,256]{1,0:T(8,128)(2,1)S(1)}, bf16[256,256]{1,0:T(8,128)(2,1)S(1)}, u32[]{:S(2)}, u32[]{:S(2)}) collective-permute-start(bf16[256,256]{1,0:T(8,128)(2,1)S(1)} %constant_dynamic-update-slice_fusion), channel_id=1, source_target_pairs={{0,16},{8,24},{16,0},{24,8},{1,17},{9,25},{17,1},{25,9},{2,18},{10... | collective-permute-start | bytes 393224 | tf_op jit(solution)/shard_map/ppermute | solution.py:31
  48.1 10.6 %collective-permute-start.5 = (bf16[256,256]{1,0:T(8,128)(2,1)S(1)}, bf16[256,256]{1,0:T(8,128)(2,1)S(1)}, u32[]{:S(2)}, u32[]{:S(2)}) collective-permute-start(bf16[256,256]{1,0:T(8,128)(2,1)S(1)} %constant_dynamic-update-slice_fusion), channel_id=1, source_target_pairs={{0,24},{8,0},{16,8},{24,16},{1,25},{9,1},{17,9},{25,17},{2,26},{10... | collective-permute-start | bytes 393224 | tf_op jit(solution)/shard_map/ppermute | solution.py:31
  58.8 6.2 %copy-start.3 = (bf16[4,256,256]{2,1,0:T(8,128)(2,1)}, bf16[4,256,256]{2,1,0:T(8,128)(2,1)S(1)}, u32[]{:S(2)}) copy-start(bf16[4,256,256]{2,1,0:T(8,128)(2,1)S(1)} %pad_maximum_fusion.own) | copy-start | bytes 1572868
  58.8 6.2 %collective-permute-start.6 = (bf16[4,256,256]{2,1,0:T(8,128)(2,1)S(1)}, bf16[4,256,256]{2,1,0:T(8,128)(2,1)S(1)}, u32[]{:S(2)}, u32[]{:S(2)}) collective-permute-start(bf16[4,256,256]{2,1,0:T(8,128)(2,1)S(1)} %pad_maximum_fusion.own), channel_id=1, source_target_pairs={{0,4},{4,0},{1,5},{5,1},{2,6},{6,2},{3,7},{7,3},{8,12},{12,8},{9,1... | collective-permute-start | bytes 1572872 | tf_op jit(solution)/shard_map/ppermute | solution.py:31
  65.0 0.8 copy-start.5
  69.3 13.6 %all-to-all-start.1 = ((f32[4,128,256]{2,1,0:T(8,128)}), f32[4,128,256]{2,1,0:T(8,128)S(1)}, u32[]{:S(2)}, u32[]{:S(2)}) async-start(f32[4,128,256]{2,1,0:T(8,128)} %project.1), calls=%async_computation.1 | async-start | bytes 1048576 | tf_op jit(solution)/shard_map/all_to_all | solution.py:216
  82.9 0.8 copy-start.2
  85.5 14.9 %collective-permute-start.7 = (bf16[128,256]{1,0:T(8,128)(2,1)}, bf16[128,256]{1,0:T(8,128)(2,1)S(1)}, u32[]{:S(2)}, u32[]{:S(2)}) collective-permute-start(bf16[128,256]{1,0:T(8,128)(2,1)} %rope.1), channel_id=1, source_target_pairs={{0,280},{1,344},{2,408},{3,472},{8,312},{9,376},{10,440},{11,504},... | collective-permute-start | bytes 196616 | tf_op jit(solution)/shard_map/ppermute | solution.py:31
  87.7 14.3 %collective-permute-start.8 = (bf16[128,256]{1,0:T(8,128)(2,1)}, bf16[128,256]{1,0:T(8,128)(2,1)S(1)}, u32[]{:S(2)}, u32[]{:S(2)}) collective-permute-start(bf16[128,256]{1,0:T(8,128)(2,1)} %rope.1), channel_id=1, source_target_pairs={{0,312},{1,376},{2,440},{3,504},{8,280},{9,344},{10,408},{11,472},... | collective-permute-start | bytes 196616 | tf_op jit(solution)/shard_map/ppermute | solution.py:31
  102.0 9.4 %collective-permute-start.9 = (bf16[256,256]{1,0:T(8,128)(2,1)S(1)}, bf16[256,256]{1,0:T(8,128)(2,1)S(1)}, u32[]{:S(2)}, u32[]{:S(2)}) collective-permute-start(bf16[256,256]{1,0:T(8,128)(2,1)S(1)} %constant_dynamic-update-slice_fusion.2), channel_id=1, source_target_pairs={{0,8},{8,16},{16,24},{24,0},{1,9},{9,17},{17,25},{25,1},{2,10},{10... | collective-permute-start | bytes 393224 | tf_op jit(solution)/shard_map/ppermute | solution.py:31
  105.4 10.8 %collective-permute-start.10 = (bf16[256,256]{1,0:T(8,128)(2,1)S(1)}, bf16[256,256]{1,0:T(8,128)(2,1)S(1)}, u32[]{:S(2)}, u32[]{:S(2)}) collective-permute-start(bf16[256,256]{1,0:T(8,128)(2,1)S(1)} %constant_dynamic-update-slice_fusion.2), channel_id=1, source_target_pairs={{0,16},{8,24},{16,0},{24,8},{1,17},{9,25},{17,1},{25,9},{2,18},{10... | collective-permute-start | bytes 393224 | tf_op jit(solution)/shard_map/ppermute | solution.py:31
  108.2 8.7 %collective-permute-start.11 = (bf16[256,256]{1,0:T(8,128)(2,1)S(1)}, bf16[256,256]{1,0:T(8,128)(2,1)S(1)}, u32[]{:S(2)}, u32[]{:S(2)}) collective-permute-start(bf16[256,256]{1,0:T(8,128)(2,1)S(1)} %constant_dynamic-update-slice_fusion.2), channel_id=1, source_target_pairs={{0,24},{8,0},{16,8},{24,16},{1,25},{9,1},{17,9},{25,17},{2,26},{10... | collective-permute-start | bytes 393224 | tf_op jit(solution)/shard_map/ppermute | solution.py:31
  117.0 7.0 %copy-start.4 = (bf16[4,256,256]{2,1,0:T(8,128)(2,1)}, bf16[4,256,256]{2,1,0:T(8,128)(2,1)S(1)}, u32[]{:S(2)}) copy-start(bf16[4,256,256]{2,1,0:T(8,128)(2,1)S(1)} %pad_maximum_fusion.1.own) | copy-start | bytes 1572868
  117.0 7.0 %collective-permute-start.12 = (bf16[4,256,256]{2,1,0:T(8,128)(2,1)S(1)}, bf16[4,256,256]{2,1,0:T(8,128)(2,1)S(1)}, u32[]{:S(2)}, u32[]{:S(2)}) collective-permute-start(bf16[4,256,256]{2,1,0:T(8,128)(2,1)S(1)} %pad_maximum_fusion.1.own), channel_id=1, source_target_pairs={{0,4},{4,0},{1,5},{5,1},{2,6},{6,2},{3,7},{7,3},{8,12},{12,8},{9,1... | collective-permute-start | bytes 1572872 | tf_op jit(solution)/shard_map/ppermute | solution.py:31
  124.0 0.8 copy-start.6
  (2 other events, 1.2 us)
Sparse Core Ops, SparseCore 0:
  10.1 42.1 all-gather.4
  54.4 30.9 all-gather.2

commit v2 on v1

v2 whole, which is shorter than its diff:
```python
import functools
import math

import jax
import jax.numpy as jnp
import numpy as np
from jax import lax
from jax.experimental import pallas as pl
from jax.experimental.pallas import tpu as pltpu
from jax.sharding import Mesh
from jax.sharding import PartitionSpec as P

HD = 128
HEADS = 8
NORM_EPS = 1e-05
ROPE_BASE = 500000.0
NEG = -1e30
SIZES = {"pipe": 2, "y": 4, "zg": 2, "zi": 4, "core": 2, "tp": 4}
AXES = tuple(SIZES)
CTX = ("y", "zg", "zi", "core")
KEY_TILE = 512
VMEM_LIMIT = 56 * 1024 * 1024


def permute(x, axes, move):
    sizes = [SIZES[a] for a in axes]
    pairs = []
    for i in range(int(np.prod(sizes))):
        at = [int(v) for v in np.unravel_index(i, sizes)]
        to = [int(v) % n for v, n in zip(move(*at), sizes)]
        pairs.append((i, int(np.ravel_multi_index(to, sizes))))
    return lax.ppermute(x, axes if len(axes) > 1 else axes[0], pairs)


TAKES = (
    (3, 5, 7, 0, 6, 1, 2, 4),
    (2, 4, 6, 1, 7, 0, 3, 5),
)


def stack_kernel(*refs):
    out = refs[-1]
    for k in range(4):
        out[k] = refs[k][...]


def join_kernel(*refs):
    out = refs[-1]
    out[:128] = refs[0][...]
    out[128:] = refs[1][...]


def spread(unit, early, late):
    pair = []
    for takes in TAKES:
        pair.append(
            permute(
                unit,
                ("pipe", "y", "zg", "zi", "tp"),
                lambda p, y, g, i, t, takes=takes: (
                    1 - p,
                    t,
                    takes.index(4 * g + i) // 4,
                    takes.index(4 * g + i) % 4,
                    y,
                ),
            )
        )
    pair = pl.pallas_call(
        join_kernel,
        out_shape=pltpu.VMEM((256, 256), jnp.bfloat16),
        in_specs=[VMEM] * (2 + len(early)),
        out_specs=VMEM,
        compiler_params=params(),
        name="join",
    )(*near(*pair, *early))
    late = late(pair)
    parts = [pair] + [permute(pair, ("zi",), lambda i, k=k: (i + k,)) for k in (1, 2, 3)]
    own = pl.pallas_call(
        stack_kernel,
        out_shape=pltpu.VMEM((4, 256, 256), jnp.bfloat16),
        in_specs=[VMEM] * (4 + len(late)),
        out_specs=VMEM,
        compiler_params=params(),
        name="stack",
    )(*near(*parts, *late))
    other = permute(own, ("core",), lambda c: (c + 1,))
    return own, other, late


def squares_kernel(acts, after, out):
    del after
    rows = acts[...].astype(jnp.float32)
    total = jnp.sum(rows * rows, axis=1, keepdims=True)
    line = jnp.transpose(jnp.broadcast_to(total, (128, 128)))[:8]
    for i in range(16):
        out[i] = line


def project_kernel(where, acts0, acts1, acts2, acts3, sums, gain, own, other, out, weight):
    for from_other, ref in enumerate((own, other)):
        for k in range(4):
            for u in range(2):
                at = where[from_other * 8 + k * 2 + u]
                weight[pl.ds(pl.multiple_of(at * 128, 128), 128), :] = ref[k, u * 128 : (u + 1) * 128, :]
    for k, acts in enumerate((acts0, acts1, acts2, acts3)):
        y = where[16 + k]
        total = (sums[4 * y] + sums[4 * y + 1]) + (sums[4 * y + 2] + sums[4 * y + 3])
        scale = lax.rsqrt(total * (1.0 / 8192) + NORM_EPS)
        column = jnp.transpose(jnp.broadcast_to(scale[:1], (128, 128)))
        normed = acts[...].astype(jnp.float32) * column[:, :1] * gain[...]
        out[y] = jnp.dot(normed.astype(jnp.bfloat16), weight[...], preferred_element_type=jnp.float32)


def rope_kernel(meta, parts, cos, sin, out):
    del meta
    total = (parts[0] + parts[1]) + (parts[2] + parts[3])
    raw = total[:, :HD]
    turned = pltpu.roll(raw, HD // 2, 1)
    out[:, :HD] = (raw * cos[...] + turned * sin[...]).astype(jnp.bfloat16)
    out[:, HD:] = total[:, HD:].astype(jnp.bfloat16)


def sort_blocks(meta, own, other, k_s, v_s):
    v_s[:, HD:] = jnp.ones((2048, HD), jnp.bfloat16)
    for from_other, ref in enumerate((own, other)):
        for k in range(4):
            for b in range(4):
                at = pl.multiple_of(meta[from_other * 16 + k * 4 + b] * 64, 64)
                k_s[pl.ds(at, 64), :] = ref[k, b * 64 : (b + 1) * 64, :HD]
                v_s[pl.ds(at, 64), :HD] = ref[k, b * 64 : (b + 1) * 64, HD:]


def attend(slot, meta, q_ref, k_s, v_s, out, s_buf, q_s, top, acc):
    rows = HEADS * 64
    factor = math.log2(math.e) / math.sqrt(HD)
    per_tile = KEY_TILE // 64
    lane = lax.broadcasted_iota(jnp.int32, (64, 128), 1)
    for half in range(2):
        here = slice(half * 64, (half + 1) * 64)
        before = meta[32 + slot * 2 + half]
        has_own = meta[40 + slot * 2 + half]
        full = before // per_tile
        left = (before - full * per_tile) * 64
        extra = jnp.minimum(left + has_own, 1)

        @pl.when(before + has_own == 0)
        def _():
            out[here, : HEADS * HD] = jnp.zeros((64, HEADS * HD), jnp.bfloat16)
            out[here, HEADS * HD :] = jnp.where(lane < HEADS, NEG, 0.0).astype(jnp.bfloat16)

        @pl.when(before + has_own > 0)
        def _():
            for h in range(HEADS):
                q_s[h * 64 : (h + 1) * 64, :] = q_ref[here, h * HD : (h + 1) * HD]
            top[...] = jnp.full(top.shape, NEG, jnp.float32)
            acc[...] = jnp.zeros(acc.shape, jnp.float32)

            def scores(t, masked):
                keys = k_s[pl.ds(pl.multiple_of(t * KEY_TILE, KEY_TILE), KEY_TILE), :]
                s = lax.dot_general(
                    q_s[...], keys, (((1,), (1,)), ((), ())), preferred_element_type=jnp.float32
                )
                if masked:
                    row = lax.broadcasted_iota(jnp.int32, (rows, KEY_TILE), 0) & 63
                    limit = left + has_own * (row + 1)
                    s = jnp.where(lax.broadcasted_iota(jnp.int32, (rows, KEY_TILE), 1) < limit, s, NEG)
                s_buf[t] = s
                best = top[...]
                for j in range(KEY_TILE // 128):
                    best = jnp.maximum(best, s[:, j * 128 : (j + 1) * 128])
                top[...] = best

            def whole(t, carry):
                scores(t, False)
                return carry

            lax.fori_loop(0, full, whole, 0)

            @pl.when(extra > 0)
            def _():
                scores(full, True)

            best = jnp.max(top[...], axis=1, keepdims=True) * factor
            top[...] = jnp.broadcast_to(best, top.shape)

            def gather(t, carry):
                best = top[...]
                p = jnp.concatenate(
                    [
                        jnp.exp2(s_buf[t, :, j * 128 : (j + 1) * 128] * factor - best).astype(jnp.bfloat16)
                        for j in range(KEY_TILE // 128)
                    ],
                    axis=1,
                )
                values = v_s[pl.ds(pl.multiple_of(t * KEY_TILE, KEY_TILE), KEY_TILE), :]
                acc[...] += jnp.dot(p, values, preferred_element_type=jnp.float32)
                return carry

            lax.fori_loop(0, full + extra, gather, 0)

            stats = jnp.zeros((64, 128), jnp.float32)
            for h in range(HEADS):
                part = slice(h * 64, (h + 1) * 64)
                total = acc[part, HD:]
                out[here, h * HD : (h + 1) * HD] = (acc[part, :HD] / total).astype(jnp.bfloat16)
                lse = top[part] * math.log(2.0) + jnp.log(total)
                high = lse.astype(jnp.bfloat16).astype(jnp.float32)
                rest = lse - high
                middle = rest.astype(jnp.bfloat16).astype(jnp.float32)
                stats = jnp.where(lane == h, high, stats)
                stats = jnp.where(lane == 8 + h, middle, stats)
                stats = jnp.where(lane == 16 + h, rest - middle, stats)
            out[here, HEADS * HD :] = stats.astype(jnp.bfloat16)


def attend_first_kernel(slot, meta, q_ref, own, other, out, k_s, v_s, *scratch):
    sort_blocks(meta, own, other, k_s, v_s)
    attend(slot, meta, q_ref, k_s, v_s, out, *scratch)


def attend_next_kernel(slot, meta, q_ref, k_s, v_s, out, *scratch):
    attend(slot, meta, q_ref, k_s, v_s, out, *scratch)


def merge_kernel(first, second, third, fourth, out, log_total):
    parts = (first, second, third, fourth)
    logs = []
    for part in parts:
        pieces = part[:, HEADS * HD :].astype(jnp.float32)
        logs.append((pieces + pltpu.roll(pieces, 120, 1)) + pltpu.roll(pieces, 112, 1))
    top = jnp.maximum(jnp.maximum(logs[0], logs[1]), jnp.maximum(logs[2], logs[3]))
    weights = [jnp.exp(v - top) for v in logs]
    total = (weights[0] + weights[1]) + (weights[2] + weights[3])
    log_total[...] = jnp.transpose(top + jnp.log(total))[:HEADS]
    weights = [w / total for w in weights]
    for h in range(HEADS):
        cols = slice(h * HD, (h + 1) * HD)
        acc = weights[0][:, h : h + 1] * parts[0][:, cols].astype(jnp.float32)
        for i in range(1, 4):
            acc = acc + weights[i][:, h : h + 1] * parts[i][:, cols].astype(jnp.float32)
        out[:, cols] = acc.astype(jnp.bfloat16)


def near(*arrays):
    return [pltpu.with_memory_space_constraint(x, pltpu.VMEM) for x in arrays]


def params(**kw):
    return pltpu.CompilerParams(vmem_limit_bytes=VMEM_LIMIT, **kw)


SMEM = pl.BlockSpec(memory_space=pltpu.SMEM)
VMEM = pl.BlockSpec(memory_space=pltpu.VMEM)


def body(section_output, norm_gain, kv_weight, queries, rank_block):
    y, g, i = lax.axis_index("y"), lax.axis_index("zg"), lax.axis_index("zi")
    c, t = lax.axis_index("core"), lax.axis_index("tp")
    z = g * 4 + i
    acts = section_output[0]
    k_index = jnp.arange(4, dtype=jnp.int32)

    acts_y = [acts] + [permute(acts, ("y",), lambda r, k=k: (r + k,)) for k in (1, 2, 3)]

    def square_sums(after):
        squares = pl.pallas_call(
            squares_kernel,
            out_shape=pltpu.VMEM((16, 8, 128), jnp.float32),
            in_specs=[VMEM] * 2,
            out_specs=VMEM,
            compiler_params=params(),
            name="squares",
        )(acts, *near(after))
        return (lax.all_to_all(squares, ("y", "tp"), 0, 0, tiled=True), *acts_y[1:])

    gain = lax.dynamic_slice(norm_gain, (0, t * 2048), (1, 2048))
    gain = permute(gain, ("pipe", "zg", "zi"), lambda p, a, b: (1 - p, 1 - a, 3 - b))
    w_own, w_other, (sums, *_) = spread(kv_weight[0], (gain,), square_sums)

    at = 4 * g + (i - k_index) % 4
    from_z = jnp.stack([jnp.array(takes, jnp.int32)[at] for takes in TAKES], axis=1).reshape(-1)
    places = jnp.concatenate([2 * from_z + c, 2 * from_z + 1 - c])
    rows_of = (y - k_index) % 4

    partial = pl.pallas_call(
        project_kernel,
        out_shape=pltpu.VMEM((4, 128, 256), jnp.float32),
        in_specs=[SMEM] + [VMEM] * 8,
        out_specs=VMEM,
        scratch_shapes=[pltpu.VMEM((2048, 256), jnp.bfloat16)],
        compiler_params=params(),
        name="project",
    )(jnp.concatenate([places, rows_of]), *near(*acts_y, sums, gain, w_own, w_other))
    parts = lax.all_to_all(partial, "tp", 0, 0, tiled=True)

    halves = jnp.arange(2, dtype=jnp.int32)[None, :]
    ids = rank_block[(2 * (16 * y + places)[:, None] + halves).reshape(-1)]
    order = jnp.sum((ids[None, :] < ids[:, None]).astype(jnp.int32), axis=1)
    q_ids = rank_block[(2 * (16 * rows_of + 2 * z + c)[:, None] + halves).reshape(-1)]
    before = jnp.sum((ids[None, :] < q_ids[:, None]).astype(jnp.int32), axis=1)
    has_own = jnp.sum((ids[None, :] == q_ids[:, None]).astype(jnp.int32), axis=1)
    meta = jnp.concatenate([order, before, has_own])

    half_row = jnp.arange(128, dtype=jnp.int32)
    blocks = lax.dynamic_slice(rank_block, (2 * (16 * t + 2 * z + c),), (2,))
    pos = jnp.where(half_row < 64, blocks[0], blocks[1]) * 64 + (half_row & 63)
    inv_freq = jnp.exp(jnp.arange(HD // 2, dtype=jnp.float32) * (-2.0 / HD) * math.log(ROPE_BASE))
    angles = pos.astype(jnp.float32)[:, None] * inv_freq[None, :]
    cos, sin = jnp.cos(angles), jnp.sin(angles)
    cos = jnp.concatenate([cos, cos], axis=1)
    sin = jnp.concatenate([-sin, sin], axis=1)
    unit = pl.pallas_call(
        rope_kernel,
        out_shape=pltpu.VMEM((128, 256), jnp.bfloat16),
        in_specs=[SMEM] + [VMEM] * 3,
        out_specs=VMEM,
        compiler_params=params(),
        name="rope",
    )(meta, *near(parts, cos, sin))
    own_q = lax.optimization_barrier((queries[0], w_other))[0]
    q_y = [own_q] + [permute(own_q, ("y",), lambda r, k=k: (r + k,)) for k in (1, 2, 3)]
    kv_own, kv_other, _ = spread(unit, q_y[1:], lambda pair: ())

    rows = HEADS * 64
    width = HEADS * HD + 128
    share = pltpu.VMEM((128, width), jnp.bfloat16)
    tables = (pltpu.VMEM((2048, HD), jnp.bfloat16), pltpu.VMEM((2048, 2 * HD), jnp.bfloat16))
    scratch = [
        pltpu.VMEM((2048 // KEY_TILE, rows, KEY_TILE), jnp.float32),
        pltpu.VMEM((rows, HD), jnp.bfloat16),
        pltpu.VMEM((rows, 128), jnp.float32),
        pltpu.VMEM((rows, 2 * HD), jnp.float32),
    ]
    shares = []
    for k in (2, 1, 3, 0):
        if k == 2:
            mine, *sorted_kv = pl.pallas_call(
                functools.partial(attend_first_kernel, k),
                out_shape=(share, *tables),
                in_specs=[SMEM] + [VMEM] * 3,
                out_specs=(VMEM,) * 3,
                scratch_shapes=scratch,
                compiler_params=params(),
                name=f"attend{k}",
            )(meta, *near(q_y[k], kv_own, kv_other))
        else:
            mine = pl.pallas_call(
                functools.partial(attend_next_kernel, k),
                out_shape=share,
                in_specs=[SMEM] + [VMEM] * 3,
                out_specs=VMEM,
                scratch_shapes=scratch,
                compiler_params=params(),
                name=f"attend{k}",
            )(meta, *near(q_y[k], *sorted_kv))
        shares.append(permute(mine, ("y",), lambda r, k=k: (r - k,)) if k else mine)
    attention, log_total = pl.pallas_call(
        merge_kernel,
        out_shape=(
            jax.ShapeDtypeStruct((128, HEADS * HD), jnp.bfloat16),
            jax.ShapeDtypeStruct((HEADS, 128), jnp.float32),
        ),
        in_specs=[VMEM] * 4,
        out_specs=(VMEM, VMEM),
        compiler_params=params(),
        name="merge",
    )(*near(*shares))
    return attention[None], jnp.transpose(log_total)[None]


def solution(mesh):
    fine = Mesh(mesh.devices.reshape(tuple(SIZES.values())), AXES)
    split = P("pipe", CTX, "tp")
    return jax.shard_map(
        body,
        mesh=fine,
        in_specs=(split, P("pipe", None), split, split, P()),
        out_specs=(split, split),
        check_vma=False,
    )
```

time: 192 us -> 180 us (0.938)
  the two profiles are of different devices: /device:TPU:129 before, /device:TPU:1 now
where the time goes in v2:
time: 180 us; the launch traced here: 178 us
  starting transfers between devices  121 us (67%)
  Pallas kernels  23.6 us (13%)
  waiting for transfers between devices  23.2 us (13%)
  local copies, waits for them, and re-layouts  5.28 us (3%)
  other arithmetic  3.52 us (2%)
    ppermute x22, starting transfers between devices, permute(): return lax.ppermute(x, axes if len(axes) > 1 else axes[0], pairs)  112 us
    ppermute x22, waiting for transfers between devices, permute(): return lax.ppermute(x, axes if len(axes) > 1 else axes[0], pairs)  17.2 us
    pallas_call x3, Pallas kernels, body(): pl.pallas_call(functools.partial(attend_next_kernel, k), out_shape=share,...  12.8 us
    all_to_all x1, waiting for transfers between devices, square_sums(): return (lax.all_to_all(squares, ('y', 'tp'), 0, 0, tiled=True), *acts_y[1:])  5.93 us
    all_to_all x1, starting transfers between devices, square_sums(): return (lax.all_to_all(squares, ('y', 'tp'), 0, 0, tiled=True), *acts_y[1:])  5.56 us
    pallas_call x1, Pallas kernels, body(): pl.pallas_call(functools.partial(attend_first_kernel, k), out_shape=(shar...  4.09 us
  transfers between devices with their start and end apart: 24, of which 7 were waited for; matrix products, arithmetic and copies ran while one was open for 4% of the time, Pallas kernels for 7%

profile of v2, /device:TPU:1, one launch (start us, length us, event | category | flops | bytes accessed | tf_op | source)
XLA Modules:
  0.0 177.7 jit_solution(14692758336003644556)
XLA Ops:
  0.6 12.8 %collective-permute-start.1 = (bf16[128,256]{1,0:T(8,128)(2,1)}, bf16[128,256]{1,0:T(8,128)(2,1)S(1)}, u32[]{:S(2)}, u32[]{:S(2)}) collective-permute-start(bf16[128,256]{1,0:T(8,128)(2,1)} %bitcast.29), channel_id=1, source_target_pairs={{0,296},{1,360},{2,424},{3,488},{8,280},{9,344},{10,408},{11,472},... | collective-permute-start | bytes 196616 | tf_op jit(solution)/shard_map/ppermute | solution.py:32
  13.5 4.7 %collective-permute-start = (bf16[128,256]{1,0:T(8,128)(2,1)}, bf16[128,256]{1,0:T(8,128)(2,1)S(1)}, u32[]{:S(2)}, u32[]{:S(2)}) collective-permute-start(bf16[128,256]{1,0:T(8,128)(2,1)} %bitcast.30), channel_id=1, source_target_pairs={{0,280},{1,344},{2,408},{3,472},{8,296},{9,360},{10,424},{11,488},... | collective-permute-start | bytes 196616 | tf_op jit(solution)/shard_map/ppermute | solution.py:32
  18.2 8.9 %collective-permute-start.8 = (bf16[128,2048]{1,0:T(8,128)(2,1)}, bf16[128,2048]{1,0:T(8,128)(2,1)S(1)}, u32[]{:S(2)}, u32[]{:S(2)}) collective-permute-start(bf16[128,2048]{1,0:T(8,128)(2,1)} %bitcast.17), channel_id=1, source_target_pairs={{0,192},{64,0},{128,64},{192,128},{1,193},{65,1},{129,65},{193,129... | collective-permute-start | bytes 1572872 | tf_op jit(solution)/shard_map/ppermute | solution.py:32
  29.8 5.2 %collective-permute-start.2 = (f32[1,2048]{1,0:T(1,128)S(1)}, f32[1,2048]{1,0:T(1,128)S(1)}, u32[]{:S(2)}, u32[]{:S(2)}) collective-permute-start(f32[1,2048]{1,0:T(1,128)S(1)} %constant_dynamic-slice_fusion), channel_id=1, source_target_pairs={{0,312},{8,304},{16,296},{24,288},{32,280},{40,272},{48,264},{56,2... | collective-permute-start | bytes 24584 | tf_op jit(solution)/shard_map/ppermute | solution.py:32
  41.9 6.7 %collective-permute-start.5 = (bf16[256,256]{1,0:T(8,128)(2,1)S(1)}, bf16[256,256]{1,0:T(8,128)(2,1)S(1)}, u32[]{:S(2)}, u32[]{:S(2)}) collective-permute-start(bf16[256,256]{1,0:T(8,128)(2,1)S(1)} %join.2.after.refs_0_), channel_id=1, source_target_pairs={{0,24},{8,0},{16,8},{24,16},{1,25},{9,1},{17,9},{25,17},{2,26},{10... | collective-permute-start | bytes 393224 | tf_op jit(solution)/shard_map/ppermute | solution.py:32
  55.6 5.6 %all-to-all-start = ((f32[16,8,128]{2,1,0:T(8,128)}), f32[16,8,128]{2,1,0:T(8,128)S(1)}, u32[]{:S(2)}, u32[]{:S(2)}) async-start(f32[16,8,128]{2,1,0:T(8,128)} %squares.1), calls=%async_computation | async-start | bytes 131072 | tf_op jit(solution)/shard_map/all_to_all | solution.py:275
  61.8 5.9 %all-to-all-done.refs_4_.sums = f32[16,8,128]{2,1,0:T(8,128)S(1)} async-done(((f32[16,8,128]{2,1,0:T(8,128)}), f32[16,8,128]{2,1,0:T(8,128)S(1)}, u32[]{:S(2)}, u32[]{:S(2)}) %all-to-all-start) | async-done | bytes 65568 | tf_op jit(solution)/shard_map/all_to_all | solution.py:275
  67.8 6.9 %collective-permute-start.9 = (bf16[4,256,256]{2,1,0:T(8,128)(2,1)S(1)}, bf16[4,256,256]{2,1,0:T(8,128)(2,1)S(1)}, u32[]{:S(2)}, u32[]{:S(2)}) collective-permute-start(bf16[4,256,256]{2,1,0:T(8,128)(2,1)S(1)} %stack.14.own), channel_id=1, source_target_pairs={{0,4},{4,0},{1,5},{5,1},{2,6},{6,2},{3,7},{7,3},{8,12},{12,8},{9,1... | collective-permute-start | bytes 1572872 | tf_op jit(solution)/shard_map/ppermute | solution.py:32
  78.7 3.5 %all-to-all-start.1 = ((f32[4,128,256]{2,1,0:T(8,128)}), f32[4,128,256]{2,1,0:T(8,128)S(1)}, u32[]{:S(2)}, u32[]{:S(2)}) async-start(f32[4,128,256]{2,1,0:T(8,128)} %project.1), calls=%async_computation.1 | async-start | bytes 1048576 | tf_op jit(solution)/shard_map/all_to_all | solution.py:295
  88.4 2.8 %collective-permute-start.10 = (bf16[128,1024]{1,0:T(8,128)(2,1)S(1)}, bf16[128,1024]{1,0:T(8,128)(2,1)S(1)}, u32[]{:S(2)}, u32[]{:S(2)}) collective-permute-start(bf16[128,1024]{1,0:T(8,128)(2,1)S(1)} %bitcast.24), channel_id=1, source_target_pairs={{0,128},{64,192},{128,0},{192,64},{1,129},{65,193},{129,1},{193,65... | collective-permute-start | bytes 786440 | tf_op jit(solution)/shard_map/ppermute | solution.py:32
  92.7 5.5 %collective-permute-start.12 = (bf16[128,256]{1,0:T(8,128)(2,1)S(1)}, bf16[128,256]{1,0:T(8,128)(2,1)S(1)}, u32[]{:S(2)}, u32[]{:S(2)}) collective-permute-start(bf16[128,256]{1,0:T(8,128)(2,1)S(1)} %rope.1), channel_id=1, source_target_pairs={{0,296},{1,360},{2,424},{3,488},{8,280},{9,344},{10,408},{11,472},... | collective-permute-start | bytes 196616 | tf_op jit(solution)/shard_map/ppermute | solution.py:32
  98.2 4.6 %collective-permute-start.11 = (bf16[128,256]{1,0:T(8,128)(2,1)S(1)}, bf16[128,256]{1,0:T(8,128)(2,1)S(1)}, u32[]{:S(2)}, u32[]{:S(2)}) collective-permute-start(bf16[128,256]{1,0:T(8,128)(2,1)S(1)} %rope.1), channel_id=1, source_target_pairs={{0,280},{1,344},{2,408},{3,472},{8,296},{9,360},{10,424},{11,488},... | collective-permute-start | bytes 196616 | tf_op jit(solution)/shard_map/ppermute | solution.py:32
  104.8 7.0 %collective-permute-done.11.refs_0_ = bf16[128,256]{1,0:T(8,128)(2,1)S(1)} collective-permute-done((bf16[128,256]{1,0:T(8,128)(2,1)S(1)}, bf16[128,256]{1,0:T(8,128)(2,1)S(1)}, u32[]{:S(2)}, u32[]{:S(2)}) %collective-permute-start.11) | collective-permute-done | bytes 65568 | tf_op jit(solution)/shard_map/ppermute | solution.py:32
  111.8 4.1 %collective-permute-start.17 = (bf16[256,256]{1,0:T(8,128)(2,1)S(1)}, bf16[256,256]{1,0:T(8,128)(2,1)S(1)}, u32[]{:S(2)}, u32[]{:S(2)}) collective-permute-start(bf16[256,256]{1,0:T(8,128)(2,1)S(1)} %join.3.refs_0_), channel_id=1, source_target_pairs={{0,24},{8,0},{16,8},{24,16},{1,25},{9,1},{17,9},{25,17},{2,26},{10... | collective-permute-start | bytes 393224 | tf_op jit(solution)/shard_map/ppermute | solution.py:32
  115.9 3.0 %collective-permute-start.16 = (bf16[256,256]{1,0:T(8,128)(2,1)S(1)}, bf16[256,256]{1,0:T(8,128)(2,1)S(1)}, u32[]{:S(2)}, u32[]{:S(2)}) collective-permute-start(bf16[256,256]{1,0:T(8,128)(2,1)S(1)} %join.3.refs_0_), channel_id=1, source_target_pairs={{0,16},{8,24},{16,0},{24,8},{1,17},{9,25},{17,1},{25,9},{2,18},{10... | collective-permute-start | bytes 393224 | tf_op jit(solution)/shard_map/ppermute | solution.py:32
  119.0 3.4 %collective-permute-start.15 = (bf16[256,256]{1,0:T(8,128)(2,1)S(1)}, bf16[256,256]{1,0:T(8,128)(2,1)S(1)}, u32[]{:S(2)}, u32[]{:S(2)}) collective-permute-start(bf16[256,256]{1,0:T(8,128)(2,1)S(1)} %join.3.refs_0_), channel_id=1, source_target_pairs={{0,8},{8,16},{16,24},{24,0},{1,9},{9,17},{17,25},{25,1},{2,10},{10... | collective-permute-start | bytes 393224 | tf_op jit(solution)/shard_map/ppermute | solution.py:32
  123.9 3.1 %collective-permute-done.15.refs_1_ = bf16[256,256]{1,0:T(8,128)(2,1)S(1)} collective-permute-done((bf16[256,256]{1,0:T(8,128)(2,1)S(1)}, bf16[256,256]{1,0:T(8,128)(2,1)S(1)}, u32[]{:S(2)}, u32[]{:S(2)}) %collective-permute-start.15) | collective-permute-done | bytes 131104 | tf_op jit(solution)/shard_map/ppermute | solution.py:32
  127.0 6.9 %collective-permute-start.18 = (bf16[4,256,256]{2,1,0:T(8,128)(2,1)S(1)}, bf16[4,256,256]{2,1,0:T(8,128)(2,1)S(1)}, u32[]{:S(2)}, u32[]{:S(2)}) collective-permute-start(bf16[4,256,256]{2,1,0:T(8,128)(2,1)S(1)} %stack.15.own), channel_id=1, source_target_pairs={{0,4},{4,0},{1,5},{5,1},{2,6},{6,2},{3,7},{7,3},{8,12},{12,8},{9,1... | collective-permute-start | bytes 1572872 | tf_op jit(solution)/shard_map/ppermute | solution.py:32
  135.4 4.1 %attend2.1 = (bf16[128,1152]{1,0:T(8,128)(2,1)S(1)}, bf16[2048,128]{1,0:T(8,128)(2,1)S(1)}, bf16[2048,256]{1,0:T(8,128)(2,1)S(1)}) custom-call(s32[48]{0:T(128)} %pad_add_fusion.meta, bf16[128,1024]{1,0:T(8,128)(2,1)S(1)} %collective-permute-done.10.refs_3_.q_ref, bf16[4,256,256]{2,1,0:T(8,128)(2,1)S(1)} %stack.15.own, ...), custom_call_target="tpu_custom_call" | custom-call | tf_op jit(solution)/shard_map/attend2/pallas_call | solution.py:338
  139.5 3.9 %attend1.1 = bf16[128,1152]{1,0:T(8,128)(2,1)S(1)} custom-call(s32[48]{0:T(128)} %pad_add_fusion.meta, bf16[128,1024]{1,0:T(8,128)(2,1)S(1)} %collective-permute-done.13.refs_2_.q_ref, bf16[2048,128]{1,0:T(8,128)(2,1)S(1)} %get-tuple-element.10.k_s, bf16[2048,256]{1,0:T(8,128)(2,1)S(1)} %get-tuple-element.11.v_s), custom_call_target="tpu_custom_call" | custom-call | tf_op jit(solution)/shard_map/attend1/pallas_call | solution.py:348
  143.4 9.3 %collective-permute-start.20 = (bf16[128,1152]{1,0:T(8,128)(2,1)S(1)}, bf16[128,1152]{1,0:T(8,128)(2,1)S(1)}, u32[]{:S(2)}, u32[]{:S(2)}) collective-permute-start(bf16[128,1152]{1,0:T(8,128)(2,1)S(1)} %attend1.1), channel_id=1, source_target_pairs={{0,192},{64,0},{128,64},{192,128},{1,193},{65,1},{129,65},{193,129... | collective-permute-start | bytes 884744 | tf_op jit(solution)/shard_map/ppermute | solution.py:32
  152.7 3.2 %attend3.1 = bf16[128,1152]{1,0:T(8,128)(2,1)S(1)} custom-call(s32[48]{0:T(128)} %pad_add_fusion.meta, bf16[128,1024]{1,0:T(8,128)(2,1)S(1)} %collective-permute-done.14.refs_4_.q_ref, bf16[2048,128]{1,0:T(8,128)(2,1)S(1)} %get-tuple-element.10.k_s, bf16[2048,256]{1,0:T(8,128)(2,1)S(1)} %get-tuple-element.11.v_s), custom_call_target="tpu_custom_call" | custom-call | tf_op jit(solution)/shard_map/attend3/pallas_call | solution.py:348
  157.9 10.4 %collective-permute-start.19 = (bf16[128,1152]{1,0:T(8,128)(2,1)S(1)}, bf16[128,1152]{1,0:T(8,128)(2,1)S(1)}, u32[]{:S(2)}, u32[]{:S(2)}) collective-permute-start(bf16[128,1152]{1,0:T(8,128)(2,1)S(1)} %get-tuple-element.9), channel_id=1, source_target_pairs={{0,128},{64,192},{128,0},{192,64},{1,129},{65,193},{129,1},{193,65... | collective-permute-start | bytes 884744 | tf_op jit(solution)/shard_map/ppermute | solution.py:32
  168.3 5.7 %attend0.1.fourth = bf16[128,1152]{1,0:T(8,128)(2,1)S(1)} custom-call(s32[48]{0:T(128)} %pad_add_fusion.meta, bf16[128,1024]{1,0:T(8,128)(2,1)S(1)} %bitcast.25, bf16[2048,128]{1,0:T(8,128)(2,1)S(1)} %get-tuple-element.10.k_s, bf16[2048,256]{1,0:T(8,128)(2,1)S(1)} %get-tuple-element.11.v_s), custom_call_target="tpu_custom_call" | custom-call | tf_op jit(solution)/shard_map/attend0/pallas_call | solution.py:348
  (83 shorter events, 39.4 us)
Async XLA Ops:
  0.6 41.2 %collective-permute-start.1 = (bf16[128,256]{1,0:T(8,128)(2,1)}, bf16[128,256]{1,0:T(8,128)(2,1)S(1)}, u32[]{:S(2)}, u32[]{:S(2)}) collective-permute-start(bf16[128,256]{1,0:T(8,128)(2,1)} %bitcast.29), channel_id=1, source_target_pairs={{0,296},{1,360},{2,424},{3,488},{8,280},{9,344},{10,408},{11,472},... | collective-permute-start | bytes 196616 | tf_op jit(solution)/shard_map/ppermute | solution.py:32
  13.5 28.4 %collective-permute-start = (bf16[128,256]{1,0:T(8,128)(2,1)}, bf16[128,256]{1,0:T(8,128)(2,1)S(1)}, u32[]{:S(2)}, u32[]{:S(2)}) collective-permute-start(bf16[128,256]{1,0:T(8,128)(2,1)} %bitcast.30), channel_id=1, source_target_pairs={{0,280},{1,344},{2,408},{3,472},{8,296},{9,360},{10,424},{11,488},... | collective-permute-start | bytes 196616 | tf_op jit(solution)/shard_map/ppermute | solution.py:32
  18.2 49.5 %collective-permute-start.8 = (bf16[128,2048]{1,0:T(8,128)(2,1)}, bf16[128,2048]{1,0:T(8,128)(2,1)S(1)}, u32[]{:S(2)}, u32[]{:S(2)}) collective-permute-start(bf16[128,2048]{1,0:T(8,128)(2,1)} %bitcast.17), channel_id=1, source_target_pairs={{0,192},{64,0},{128,64},{192,128},{1,193},{65,1},{129,65},{193,129... | collective-permute-start | bytes 1572872 | tf_op jit(solution)/shard_map/ppermute | solution.py:32
  27.1 40.7 %collective-permute-start.7 = (bf16[128,2048]{1,0:T(8,128)(2,1)}, bf16[128,2048]{1,0:T(8,128)(2,1)S(1)}, u32[]{:S(2)}, u32[]{:S(2)}) collective-permute-start(bf16[128,2048]{1,0:T(8,128)(2,1)} %bitcast.18), channel_id=1, source_target_pairs={{0,128},{64,192},{128,0},{192,64},{1,129},{65,193},{129,1},{193,65... | collective-permute-start | bytes 1572872 | tf_op jit(solution)/shard_map/ppermute | solution.py:32
  29.8 9.3 %collective-permute-start.2 = (f32[1,2048]{1,0:T(1,128)S(1)}, f32[1,2048]{1,0:T(1,128)S(1)}, u32[]{:S(2)}, u32[]{:S(2)}) collective-permute-start(f32[1,2048]{1,0:T(1,128)S(1)} %constant_dynamic-slice_fusion), channel_id=1, source_target_pairs={{0,312},{8,304},{16,296},{24,288},{32,280},{40,272},{48,264},{56,2... | collective-permute-start | bytes 24584 | tf_op jit(solution)/shard_map/ppermute | solution.py:32
  39.1 28.7 %collective-permute-start.6 = (bf16[128,2048]{1,0:T(8,128)(2,1)S(1)}, bf16[128,2048]{1,0:T(8,128)(2,1)S(1)}, u32[]{:S(2)}, u32[]{:S(2)}) collective-permute-start(bf16[128,2048]{1,0:T(8,128)(2,1)S(1)} %bitcast.20), channel_id=1, source_target_pairs={{0,64},{64,128},{128,192},{192,0},{1,65},{65,129},{129,193},{193,1... | collective-permute-start | bytes 1572872 | tf_op jit(solution)/shard_map/ppermute | solution.py:32
  41.9 9.5 %collective-permute-start.5 = (bf16[256,256]{1,0:T(8,128)(2,1)S(1)}, bf16[256,256]{1,0:T(8,128)(2,1)S(1)}, u32[]{:S(2)}, u32[]{:S(2)}) collective-permute-start(bf16[256,256]{1,0:T(8,128)(2,1)S(1)} %join.2.after.refs_0_), channel_id=1, source_target_pairs={{0,24},{8,0},{16,8},{24,16},{1,25},{9,1},{17,9},{25,17},{2,26},{10... | collective-permute-start | bytes 393224 | tf_op jit(solution)/shard_map/ppermute | solution.py:32
  49.5 18.2 %collective-permute-start.4 = (bf16[256,256]{1,0:T(8,128)(2,1)S(1)}, bf16[256,256]{1,0:T(8,128)(2,1)S(1)}, u32[]{:S(2)}, u32[]{:S(2)}) collective-permute-start(bf16[256,256]{1,0:T(8,128)(2,1)S(1)} %join.2.after.refs_0_), channel_id=1, source_target_pairs={{0,16},{8,24},{16,0},{24,8},{1,17},{9,25},{17,1},{25,9},{2,18},{10... | collective-permute-start | bytes 393224 | tf_op jit(solution)/shard_map/ppermute | solution.py:32
  51.4 16.3 %collective-permute-start.3 = (bf16[256,256]{1,0:T(8,128)(2,1)S(1)}, bf16[256,256]{1,0:T(8,128)(2,1)S(1)}, u32[]{:S(2)}, u32[]{:S(2)}) collective-permute-start(bf16[256,256]{1,0:T(8,128)(2,1)S(1)} %join.2.after.refs_0_), channel_id=1, source_target_pairs={{0,8},{8,16},{16,24},{24,0},{1,9},{9,17},{17,25},{25,1},{2,10},{10... | collective-permute-start | bytes 393224 | tf_op jit(solution)/shard_map/ppermute | solution.py:32
  55.6 12.1 %all-to-all-start = ((f32[16,8,128]{2,1,0:T(8,128)}), f32[16,8,128]{2,1,0:T(8,128)S(1)}, u32[]{:S(2)}, u32[]{:S(2)}) async-start(f32[16,8,128]{2,1,0:T(8,128)} %squares.1), calls=%async_computation | async-start | bytes 131072 | tf_op jit(solution)/shard_map/all_to_all | solution.py:275
  67.8 8.5 %collective-permute-start.9 = (bf16[4,256,256]{2,1,0:T(8,128)(2,1)S(1)}, bf16[4,256,256]{2,1,0:T(8,128)(2,1)S(1)}, u32[]{:S(2)}, u32[]{:S(2)}) collective-permute-start(bf16[4,256,256]{2,1,0:T(8,128)(2,1)S(1)} %stack.14.own), channel_id=1, source_target_pairs={{0,4},{4,0},{1,5},{5,1},{2,6},{6,2},{3,7},{7,3},{8,12},{12,8},{9,1... | collective-permute-start | bytes 1572872 | tf_op jit(solution)/shard_map/ppermute | solution.py:32
  78.7 13.2 %all-to-all-start.1 = ((f32[4,128,256]{2,1,0:T(8,128)}), f32[4,128,256]{2,1,0:T(8,128)S(1)}, u32[]{:S(2)}, u32[]{:S(2)}) async-start(f32[4,128,256]{2,1,0:T(8,128)} %project.1), calls=%async_computation.1 | async-start | bytes 1048576 | tf_op jit(solution)/shard_map/all_to_all | solution.py:295
  83.1 19.7 %collective-permute-start.14 = (bf16[128,1024]{1,0:T(8,128)(2,1)S(1)}, bf16[128,1024]{1,0:T(8,128)(2,1)S(1)}, u32[]{:S(2)}, u32[]{:S(2)}) collective-permute-start(bf16[128,1024]{1,0:T(8,128)(2,1)S(1)} %bitcast.22), channel_id=1, source_target_pairs={{0,192},{64,0},{128,64},{192,128},{1,193},{65,1},{129,65},{193,129... | collective-permute-start | bytes 786440 | tf_op jit(solution)/shard_map/ppermute | solution.py:32
  85.9 17.0 %collective-permute-start.13 = (bf16[128,1024]{1,0:T(8,128)(2,1)S(1)}, bf16[128,1024]{1,0:T(8,128)(2,1)S(1)}, u32[]{:S(2)}, u32[]{:S(2)}) collective-permute-start(bf16[128,1024]{1,0:T(8,128)(2,1)S(1)} %bitcast.23), channel_id=1, source_target_pairs={{0,64},{64,128},{128,192},{192,0},{1,65},{65,129},{129,193},{193,1... | collective-permute-start | bytes 786440 | tf_op jit(solution)/shard_map/ppermute | solution.py:32
  88.4 14.4 %collective-permute-start.10 = (bf16[128,1024]{1,0:T(8,128)(2,1)S(1)}, bf16[128,1024]{1,0:T(8,128)(2,1)S(1)}, u32[]{:S(2)}, u32[]{:S(2)}) collective-permute-start(bf16[128,1024]{1,0:T(8,128)(2,1)S(1)} %bitcast.24), channel_id=1, source_target_pairs={{0,128},{64,192},{128,0},{192,64},{1,129},{65,193},{129,1},{193,65... | collective-permute-start | bytes 786440 | tf_op jit(solution)/shard_map/ppermute | solution.py:32
  92.7 12.1 %collective-permute-start.12 = (bf16[128,256]{1,0:T(8,128)(2,1)S(1)}, bf16[128,256]{1,0:T(8,128)(2,1)S(1)}, u32[]{:S(2)}, u32[]{:S(2)}) collective-permute-start(bf16[128,256]{1,0:T(8,128)(2,1)S(1)} %rope.1), channel_id=1, source_target_pairs={{0,296},{1,360},{2,424},{3,488},{8,280},{9,344},{10,408},{11,472},... | collective-permute-start | bytes 196616 | tf_op jit(solution)/shard_map/ppermute | solution.py:32
  98.2 13.6 %collective-permute-start.11 = (bf16[128,256]{1,0:T(8,128)(2,1)S(1)}, bf16[128,256]{1,0:T(8,128)(2,1)S(1)}, u32[]{:S(2)}, u32[]{:S(2)}) collective-permute-start(bf16[128,256]{1,0:T(8,128)(2,1)S(1)} %rope.1), channel_id=1, source_target_pairs={{0,280},{1,344},{2,408},{3,472},{8,296},{9,360},{10,424},{11,488},... | collective-permute-start | bytes 196616 | tf_op jit(solution)/shard_map/ppermute | solution.py:32
  111.8 10.5 %collective-permute-start.17 = (bf16[256,256]{1,0:T(8,128)(2,1)S(1)}, bf16[256,256]{1,0:T(8,128)(2,1)S(1)}, u32[]{:S(2)}, u32[]{:S(2)}) collective-permute-start(bf16[256,256]{1,0:T(8,128)(2,1)S(1)} %join.3.refs_0_), channel_id=1, source_target_pairs={{0,24},{8,0},{16,8},{24,16},{1,25},{9,1},{17,9},{25,17},{2,26},{10... | collective-permute-start | bytes 393224 | tf_op jit(solution)/shard_map/ppermute | solution.py:32
  115.9 8.0 %collective-permute-start.16 = (bf16[256,256]{1,0:T(8,128)(2,1)S(1)}, bf16[256,256]{1,0:T(8,128)(2,1)S(1)}, u32[]{:S(2)}, u32[]{:S(2)}) collective-permute-start(bf16[256,256]{1,0:T(8,128)(2,1)S(1)} %join.3.refs_0_), channel_id=1, source_target_pairs={{0,16},{8,24},{16,0},{24,8},{1,17},{9,25},{17,1},{25,9},{2,18},{10... | collective-permute-start | bytes 393224 | tf_op jit(solution)/shard_map/ppermute | solution.py:32
  119.0 8.0 %collective-permute-start.15 = (bf16[256,256]{1,0:T(8,128)(2,1)S(1)}, bf16[256,256]{1,0:T(8,128)(2,1)S(1)}, u32[]{:S(2)}, u32[]{:S(2)}) collective-permute-start(bf16[256,256]{1,0:T(8,128)(2,1)S(1)} %join.3.refs_0_), channel_id=1, source_target_pairs={{0,8},{8,16},{16,24},{24,0},{1,9},{9,17},{17,25},{25,1},{2,10},{10... | collective-permute-start | bytes 393224 | tf_op jit(solution)/shard_map/ppermute | solution.py:32
  127.0 8.4 %collective-permute-start.18 = (bf16[4,256,256]{2,1,0:T(8,128)(2,1)S(1)}, bf16[4,256,256]{2,1,0:T(8,128)(2,1)S(1)}, u32[]{:S(2)}, u32[]{:S(2)}) collective-permute-start(bf16[4,256,256]{2,1,0:T(8,128)(2,1)S(1)} %stack.15.own), channel_id=1, source_target_pairs={{0,4},{4,0},{1,5},{5,1},{2,6},{6,2},{3,7},{7,3},{8,12},{12,8},{9,1... | collective-permute-start | bytes 1572872 | tf_op jit(solution)/shard_map/ppermute | solution.py:32
  143.4 30.6 %collective-permute-start.20 = (bf16[128,1152]{1,0:T(8,128)(2,1)S(1)}, bf16[128,1152]{1,0:T(8,128)(2,1)S(1)}, u32[]{:S(2)}, u32[]{:S(2)}) collective-permute-start(bf16[128,1152]{1,0:T(8,128)(2,1)S(1)} %attend1.1), channel_id=1, source_target_pairs={{0,192},{64,0},{128,64},{192,128},{1,193},{65,1},{129,65},{193,129... | collective-permute-start | bytes 884744 | tf_op jit(solution)/shard_map/ppermute | solution.py:32
  155.9 20.2 %collective-permute-start.21 = (bf16[128,1152]{1,0:T(8,128)(2,1)S(1)}, bf16[128,1152]{1,0:T(8,128)(2,1)S(1)}, u32[]{:S(2)}, u32[]{:S(2)}) collective-permute-start(bf16[128,1152]{1,0:T(8,128)(2,1)S(1)} %attend3.1), channel_id=1, source_target_pairs={{0,64},{64,128},{128,192},{192,0},{1,65},{65,129},{129,193},{193,1... | collective-permute-start | bytes 884744 | tf_op jit(solution)/shard_map/ppermute | solution.py:32
  157.9 18.3 %collective-permute-start.19 = (bf16[128,1152]{1,0:T(8,128)(2,1)S(1)}, bf16[128,1152]{1,0:T(8,128)(2,1)S(1)}, u32[]{:S(2)}, u32[]{:S(2)}) collective-permute-start(bf16[128,1152]{1,0:T(8,128)(2,1)S(1)} %get-tuple-element.9), channel_id=1, source_target_pairs={{0,128},{64,192},{128,0},{192,64},{1,129},{65,193},{129,1},{193,65... | collective-permute-start | bytes 884744 | tf_op jit(solution)/shard_map/ppermute | solution.py:32
  (7 other events, 43.9 us)
